TPU v7x, 128 devices: a whole 4x4x4 slice. The times are simulated.
128 devices in a mesh: dp: 4 (over x), section: 2 (over core), ts: 16 (over z, y).
Axes of the slice: x: 4, y: 4, z: 4, core: 2. Of those that a mesh axis runs over, the one named last changes fastest.
Arguments:
- inputs: bfloat16 [2, 512, 4096], P(None, ('dp', 'ts')), may hold values from -6 to 6
- cotangent: bfloat16 [2, 512, 4096], P(None, ('dp', 'ts')), may hold values from -4 to 4
- gains: float32 [2, 4096], P('section'), may hold values from 0.1 to 1.9
- weights: bfloat16 [2, 3, 112, 12, 128, 128], P('section', None, 'ts'), may hold values from -0.1875 to 0.1875
- block_rows: int32 [2, 3, 112, 12], P('section', None, 'ts'), may hold values from 0 to 31, as said below
- block_count: int32 [2, 3, 112], P('section', None, 'ts'), may hold values from 4 to 12, as said below
Outputs:
- segment_outputs: bfloat16 [2, 2, 512, 4096], P('section', None, ('dp', 'ts'))
- input_grads: bfloat16 [2, 2, 512, 4096], P('section', None, ('dp', 'ts'))
- weight_grads: bfloat16 [2, 3, 112, 12, 128, 128], P('section', None, 'ts', None, 'dp')
Inputs may be any that keep to these rules, and one draw needn't show every extreme that they name: `block_rows`: within the 12 slots of one hidden block of one matrix and segment the feature blocks are distinct. `block_count`: for every segment, matrix and index of ts some hidden block has all 12 slots live.
All inputs are finite; a program needn't handle non-finite values.
Results may differ from a plain program's by a relative error of at most 0.03.
Values may be sent and summed in bfloat16 or wider, within the bound.
A program may use at most 192 MiB of HBM per device.

v0:
```python
import jax
import jax.numpy as jnp
from jax import lax
from jax.sharding import PartitionSpec as P

EPSILON = 1e-05


def passed_along(block, axis, distance):
    devices = range(lax.axis_size(axis))
    route = [(i - distance, i) for i in devices if i - distance in devices]
    return lax.ppermute(block, axis, route)


def pick_micro(store, index):
    return lax.dynamic_index_in_dim(store, index, 0, keepdims=False)


def keep_micro(store, index, active, fresh):
    older = pick_micro(store, index)
    return lax.dynamic_update_index_in_dim(store, jnp.where(active, fresh, older), index, 0)


def shards(inputs, cotangent, gains, weights, block_rows, block_count):
    segment_index = lax.axis_index("section")
    segment_count = lax.axis_size("section")
    micro_count, shard_rows, width = inputs.shape
    block = weights.shape[-1]
    row_blocks = width // block
    hidden_cols = weights.shape[2]
    slot_count = weights.shape[3]
    gathered_rows = shard_rows * lax.axis_size("ts")
    hidden_width = hidden_cols * block
    gain = gains[0]
    lists = block_rows[0]
    live = jnp.arange(slot_count)[None, None, :] < block_count[0][:, :, None]
    masked = weights[0] * live[..., None, None].astype(jnp.bfloat16)
    live_scale = live.astype(jnp.float32)[..., None, None]
    onehot = (lists[..., None] == jnp.arange(row_blocks)[None, None, None, :]).astype(jnp.bfloat16)
    placed_gate = (
        jnp.einsum("cjk,cjbn->kbcn", onehot[0], masked[0], preferred_element_type=jnp.float32)
        .astype(jnp.bfloat16)
        .reshape(width, hidden_width)
    )
    placed_up = (
        jnp.einsum("cjk,cjbn->kbcn", onehot[1], masked[1], preferred_element_type=jnp.float32)
        .astype(jnp.bfloat16)
        .reshape(width, hidden_width)
    )
    placed_down = (
        jnp.einsum("cjk,cjhd->chkd", onehot[2], masked[2], preferred_element_type=jnp.float32)
        .astype(jnp.bfloat16)
        .reshape(hidden_width, width)
    )
    tick_count = micro_count + segment_count - 1
    hidden_shape = (gathered_rows, hidden_cols, block)

    def ffn_forward(gathered):
        gate = jnp.dot(gathered, placed_gate, preferred_element_type=jnp.float32)
        upper = jnp.dot(gathered, placed_up, preferred_element_type=jnp.float32)
        hidden = (jax.nn.silu(gate) * upper).astype(jnp.bfloat16)
        branch = jnp.dot(hidden, placed_down, preferred_element_type=jnp.float32)
        return (branch, gate.reshape(hidden_shape), upper.reshape(hidden_shape))

    def ffn_spare(gathered):
        empty = jnp.zeros(hidden_shape, jnp.float32)
        return (jnp.zeros((gathered_rows, width), jnp.float32), empty, empty)

    received = jnp.zeros((shard_rows, width), jnp.bfloat16)
    outputs = jnp.zeros((micro_count, shard_rows, width), jnp.bfloat16)
    entering = jnp.zeros((micro_count, shard_rows, width), jnp.bfloat16)
    normed_store = jnp.zeros((micro_count, gathered_rows, width), jnp.bfloat16)
    gate_store = jnp.zeros((micro_count,) + hidden_shape, jnp.float32)
    upper_store = jnp.zeros((micro_count,) + hidden_shape, jnp.float32)
    for tick_step in range(tick_count):
        micro_index = tick_step - segment_index
        active = (micro_index >= 0) & (micro_index < micro_count)
        which = jnp.clip(micro_index, 0, micro_count - 1)
        act_in = jnp.where(segment_index == 0, pick_micro(inputs, which), received)
        values = act_in.astype(jnp.float32)
        scale = lax.rsqrt(jnp.mean(values * values, axis=-1, keepdims=True) + EPSILON)
        normed = (values * scale * gain).astype(jnp.bfloat16)
        gathered = lax.all_gather(normed, "ts", axis=0, tiled=True)
        branch, gate, upper = lax.cond(active, ffn_forward, ffn_spare, gathered)
        summed = lax.psum_scatter(
            branch.astype(jnp.bfloat16), "ts", scatter_dimension=0, tiled=True
        ).astype(jnp.float32)
        act_out = (values + summed).astype(jnp.bfloat16)
        outputs = keep_micro(outputs, which, active, act_out)
        entering = keep_micro(entering, which, active, act_in)
        normed_store = keep_micro(normed_store, which, active, gathered)
        gate_store = keep_micro(gate_store, which, active, gate)
        upper_store = keep_micro(upper_store, which, active, upper)
        received = passed_along(act_out, "section", 1)
    accum = jnp.zeros((), jnp.float32)

    def ffn_backward(operands):
        gathered, grad_full, gate, upper, total = operands
        d_hidden = lax.dot_general(
            grad_full, placed_down, (((1,), (1,)), ((), ())), preferred_element_type=jnp.float32
        ).reshape(hidden_shape)
        sig = jax.nn.sigmoid(gate)
        d_gate = (d_hidden * upper * sig * (1.0 + gate * (1.0 - sig))).astype(jnp.bfloat16)
        d_up = (d_hidden * gate * sig).astype(jnp.bfloat16)
        back = lax.dot_general(
            d_gate.reshape(gathered_rows, hidden_width),
            placed_gate,
            (((1,), (1,)), ((), ())),
            preferred_element_type=jnp.float32,
        )
        back = back + lax.dot_general(
            d_up.reshape(gathered_rows, hidden_width),
            placed_up,
            (((1,), (1,)), ((), ())),
            preferred_element_type=jnp.float32,
        )
        return (back, d_gate, d_up, total)

    def back_spare(operands):
        empty = jnp.zeros(hidden_shape, jnp.bfloat16)
        return (jnp.zeros((gathered_rows, width), jnp.float32), empty, empty, operands[4])

    received = jnp.zeros((shard_rows, width), jnp.bfloat16)
    in_grads = jnp.zeros((micro_count, shard_rows, width), jnp.bfloat16)
    delta_store = jnp.zeros((micro_count, gathered_rows, width), jnp.bfloat16)
    dgate_store = jnp.zeros((micro_count,) + hidden_shape, jnp.bfloat16)
    dup_store = jnp.zeros((micro_count,) + hidden_shape, jnp.bfloat16)
    for tick_step in range(tick_count):
        micro_index = tick_step - (segment_count - 1 - segment_index)
        active = (micro_index >= 0) & (micro_index < micro_count)
        which = jnp.clip(micro_index, 0, micro_count - 1)
        delta = jnp.where(
            segment_index == segment_count - 1, pick_micro(cotangent, which), received
        )
        grad_full = lax.all_gather(delta, "ts", axis=0, tiled=True)
        operands = (
            pick_micro(normed_store, which),
            grad_full,
            pick_micro(gate_store, which),
            pick_micro(upper_store, which),
            accum,
        )
        back, d_gate, d_up, accum = lax.cond(active, ffn_backward, back_spare, operands)
        d_norm = lax.psum_scatter(
            back.astype(jnp.bfloat16), "ts", scatter_dimension=0, tiled=True
        ).astype(jnp.float32)
        values = pick_micro(entering, which).astype(jnp.float32)
        scale = lax.rsqrt(jnp.mean(values * values, axis=-1, keepdims=True) + EPSILON)
        cube = scale * scale * scale
        d_input = (
            delta.astype(jnp.float32)
            + scale * gain * d_norm
            - values * cube * jnp.mean(gain * d_norm * values, axis=-1, keepdims=True)
        ).astype(jnp.bfloat16)
        in_grads = keep_micro(in_grads, which, active, d_input)
        delta_store = keep_micro(delta_store, which, active, grad_full)
        dgate_store = keep_micro(dgate_store, which, active, d_gate)
        dup_store = keep_micro(dup_store, which, active, d_up)
        received = passed_along(d_input, "section", -1)
    quarter = block // lax.axis_size("dp")
    quarter_start = lax.axis_index("dp") * quarter
    hidden_store = (jax.nn.silu(gate_store) * upper_store).astype(jnp.bfloat16)
    initial = jnp.zeros((3, hidden_cols, slot_count, quarter, block), jnp.float32)
    carry = initial
    normed_all = lax.all_gather(normed_store, "dp", axis=0, tiled=True)
    hidden_all = lax.all_gather(hidden_store, "dp", axis=0, tiled=True)
    dgate_all = lax.all_gather(dgate_store, "dp", axis=0, tiled=True)
    dup_all = lax.all_gather(dup_store, "dp", axis=0, tiled=True)
    delta_all = lax.all_gather(delta_store, "dp", axis=0, tiled=True)
    for source in range(normed_all.shape[0] // micro_count):
        low_row = source * micro_count
        high_row = low_row + micro_count
        feats = normed_all[low_row:high_row].reshape(-1, row_blocks, block)
        feats = lax.dynamic_slice_in_dim(feats, quarter_start, quarter, 2)
        hidden_part = hidden_all[low_row:high_row].reshape(-1, hidden_cols, block)
        hidden_part = lax.dynamic_slice_in_dim(hidden_part, quarter_start, quarter, 2)
        dgate_part = dgate_all[low_row:high_row].reshape(-1, hidden_cols, block)
        dup_part = dup_all[low_row:high_row].reshape(-1, hidden_cols, block)
        grad_blocks = delta_all[low_row:high_row].reshape(-1, row_blocks, block)[:, lists[2]]
        terms = jnp.stack(
            [
                jnp.einsum(
                    "rcjb,rcn->cjbn",
                    feats[:, lists[0]],
                    dgate_part,
                    preferred_element_type=jnp.float32,
                ),
                jnp.einsum(
                    "rcjb,rcn->cjbn",
                    feats[:, lists[1]],
                    dup_part,
                    preferred_element_type=jnp.float32,
                ),
                jnp.einsum(
                    "rch,rcjd->cjhd", hidden_part, grad_blocks, preferred_element_type=jnp.float32
                ),
            ]
        )
        terms = terms * live_scale
        carry = carry + terms.astype(jnp.bfloat16).astype(jnp.float32)
    return (outputs[None], in_grads[None], carry.astype(jnp.bfloat16)[None])


def solution(mesh):
    in_specs = (
        P(None, ("dp", "ts"), None),
        P(None, ("dp", "ts"), None),
        P("section", None),
        P("section", None, "ts", None, None, None),
        P("section", None, "ts", None),
        P("section", None, "ts"),
    )
    out_specs = (
        P("section", None, ("dp", "ts"), None),
        P("section", None, ("dp", "ts"), None),
        P("section", None, "ts", None, "dp", None),
    )
    return jax.shard_map(shards, mesh=mesh, in_specs=in_specs, out_specs=out_specs, check_vma=False)
```

profile of v0, /device:TPU:0, one launch (start us, length us, event | category | flops | bytes accessed | tf_op | source)
XLA Modules:
  0.0 1164.5 jit_solution(7193997720358732015)
XLA Ops:
  12.1 12.1 %bitcast_multiply_fusion.9 = bf16[3,7,12,128,128]{4,2,3,1,0:T(8,128)(2,1)} fusion(bf16[1,3,7,12,128,128]{5,4,3,2,1,0:T(8,128)(2,1)} %param.21, bf16[3,7,12]{2,1,0:T(8,128)(2,1)S(1)} %get-tuple-element.414), kind=kLoop, calls=%fused_computation.96 | loop fusion | flops 4128768 | bytes 16515576 | tf_op jit(solution)/shard_map/mul | solution.py:37
  24.1 7.0 convert_bitcast_fusion.1
  31.1 7.1 convert_bitcast_fusion
  38.3 13.1 %copy.164 = bf16[32,128,7,128]{1,0,3,2:T(8,128)(2,1)} copy(bf16[32,128,7,128]{3,0,1,2:T(8,128)(2,1)} %convert_bitcast_fusion.1) | data formatting | bytes 14680064 | tf_op jit(solution)/shard_map/convert_element_type | solution.py:42
  51.3 13.4 %copy.278 = bf16[112,8,32,128]{3,1,2,0:T(8,128)(2,1)} copy(bf16[112,8,32,128]{3,2,1,0:T(8,128)(2,1)} %bitcast.572) | data formatting | bytes 14680064
  64.8 12.9 %copy.165 = bf16[32,128,7,128]{1,0,3,2:T(8,128)(2,1)} copy(bf16[32,128,7,128]{3,0,1,2:T(8,128)(2,1)} %convert_bitcast_fusion) | data formatting | bytes 14680064 | tf_op jit(solution)/shard_map/convert_element_type | solution.py:47
  77.6 4.3 convolution_convert_fusion
  81.9 13.4 %copy_bitcast_fusion = (bf16[896,4096]{1,0:T(8,128)(2,1)}, bf16[4096,896]{0,1:T(8,128)(2,1)}) fusion(bf16[112,8,32,128]{3,2,1,0:T(8,128)(2,1)S(1)} %bitcast.571, bf16[112,8,32,128]{3,2,1,0:T(8,128)(2,1)S(1)} %bitcast.570), kind=kLoop, calls=%fused_computation.97 | loop fusion | bytes 29360128 | tf_op jit(solution)/shard_map/reshape | solution.py:53
  95.4 11.2 conditional.6
  95.4 6.0 fusion.122
  101.4 2.5 fusion.121
  109.8 87.6 %all-reduce.13.cloned.1.call-done = bf16[128,4096]{1,0:T(8,128)(2,1)} async-done(((bf16[128,4096]{1,0:T(8,128)(2,1)}), bf16[128,4096]{1,0:T(8,128)(2,1)}) %all-reduce.13.cloned.1.call-update) | async-done | bytes 1048592
  202.5 42.0 %all-gather.15.cloned.1.call-done = bf16[128,4096]{1,0:T(8,128)(2,1)} async-done(((bf16[8,4096]{1,0:T(8,128)(2,1)}), bf16[128,4096]{1,0:T(8,128)(2,1)}) %all-gather.15.cloned.1.call-update) | async-done | bytes 1048592 | tf_op jit(solution)/shard_map/all_gather | solution.py:83
  244.4 13.2 %conditional.7 = (bf16[128,4096]{1,0:T(8,128)(2,1)S(1)}, f32[128,7,128]{2,0,1:T(8,128)}, f32[128,7,128]{2,0,1:T(8,128)S(1)}) conditional(s32[]{:T(128)} %convert_element_type.325, () %tuple.70, (bf16[128,4096]{1,0:T(8,128)(2,1)}, bf16[4096,896]{0,1:T(8,128)(2,1)}, bf16[4096,896]{0,1:T(8,128)(2,1)}, bf16[896,4096]{1,0:T(8,128)(2,1)}) %tuple.194), branch_computations={%region_5.6_spmd, %region_6.7_spmd} | conditional | flops 2819260416 | bytes 95420544 | solution.py:84
  244.5 6.0 fusion.124
  250.5 2.4 fusion.123
  258.7 86.5 %all-reduce.15.cloned.1.call-done = bf16[128,4096]{1,0:T(8,128)(2,1)} async-done(((bf16[128,4096]{1,0:T(8,128)(2,1)}), bf16[128,4096]{1,0:T(8,128)(2,1)}) %all-reduce.15.cloned.1.call-update) | async-done | bytes 1048592
  360.6 30.8 %all-gather.17.cloned.1.call-done = bf16[128,4096]{1,0:T(8,128)(2,1)} async-done(((bf16[8,4096]{1,0:T(8,128)(2,1)}), bf16[128,4096]{1,0:T(8,128)(2,1)}) %all-gather.17.cloned.1.call-update) | async-done | bytes 1048592 | tf_op jit(solution)/shard_map/all_gather | solution.py:83
  394.8 40.7 %all-gather.33.cloned.1.call-done = bf16[1,128,4096]{2,1,0:T(8,128)(2,1)} async-done(((bf16[1,8,4096]{2,1,0:T(8,128)(2,1)}), bf16[1,128,4096]{2,1,0:T(8,128)(2,1)}) %all-gather.33.cloned.1.call-update) | async-done | bytes 1048592 | tf_op jit(solution)/shard_map/all_gather | solution.py:135
  435.5 2.8 conditional.9
  438.4 103.7 %all-reduce.17.cloned.1.call-done = bf16[128,4096]{1,0:T(8,128)(2,1)} async-done(((bf16[128,4096]{1,0:T(8,128)(2,1)}), bf16[128,4096]{1,0:T(8,128)(2,1)}) %all-reduce.17.cloned.1.call-update) | async-done | bytes 1048592
  549.4 42.1 %all-gather.19.cloned.1.call-done = bf16[128,4096]{1,0:T(8,128)(2,1)} async-done(((bf16[8,4096]{1,0:T(8,128)(2,1)}), bf16[128,4096]{1,0:T(8,128)(2,1)}) %all-gather.19.cloned.1.call-update) | async-done | bytes 1048592 | tf_op jit(solution)/shard_map/all_gather | solution.py:135
  591.5 21.5 %conditional.10 = (bf16[128,4096]{1,0:T(8,128)(2,1)}, bf16[128,7,128]{0,2,1:T(8,128)(2,1)}, bf16[128,7,128]{0,2,1:T(8,128)(2,1)}) conditional(s32[]{:T(128)} %convert_element_type.346, () %tuple.76, (bf16[128,4096]{1,0:T(8,128)(2,1)}, bf16[896,4096]{1,0:T(8,128)(2,1)}, f32[2,128,7,128]{3,1,2,0:T(8,128)}, s32[]{:T(128)}, ...), branch_computations={%region_18.19_spmd, %region_19.20_spmd} | conditional | flops 2823290880 | bytes 68681896 | solution.py:143
  591.5 5.9 fusion.128
  603.4 2.2 copy.153
  605.6 5.0 fusion.32
  610.6 2.3 convolution_add_fusion.1
  613.7 85.8 %all-reduce.19.cloned.1.call-done = bf16[128,4096]{1,0:T(8,128)(2,1)} async-done(((bf16[128,4096]{1,0:T(8,128)(2,1)}), bf16[128,4096]{1,0:T(8,128)(2,1)}) %all-reduce.19.cloned.1.call-update) | async-done | bytes 1048592
  706.6 2.5 multiply_convert_fusion.18
  709.2 39.1 %all-gather.21.cloned.1.call-done = bf16[128,4096]{1,0:T(8,128)(2,1)} async-done(((bf16[8,4096]{1,0:T(8,128)(2,1)}), bf16[128,4096]{1,0:T(8,128)(2,1)}) %all-gather.21.cloned.1.call-update) | async-done | bytes 1048592 | tf_op jit(solution)/shard_map/all_gather | solution.py:135
  748.3 21.5 %conditional.11 = (bf16[128,4096]{1,0:T(8,128)(2,1)}, bf16[128,7,128]{0,2,1:T(8,128)(2,1)}, bf16[128,7,128]{0,2,1:T(8,128)(2,1)}) conditional(s32[]{:T(128)} %convert_element_type.353, () %tuple.78, (bf16[128,4096]{1,0:T(8,128)(2,1)}, bf16[896,4096]{1,0:T(8,128)(2,1)}, f32[2,128,7,128]{3,1,2,0:T(8,128)}, s32[]{:T(128)}, ...), branch_computations={%region_23.24_spmd, %region_24.25_spmd} | conditional | flops 2823290880 | bytes 68681896 | solution.py:143
  748.3 5.9 fusion.129
  760.2 2.1 copy.158
  762.4 5.0 fusion.46
  767.5 2.4 convolution_add_fusion.2
  801.0 71.3 %all-reduce.21.cloned.1.call-done = (bf16[128,4096]{1,0:T(8,128)(2,1)}, bf16[128,4096]{1,0:T(8,128)(2,1)}) async-done(((bf16[128,4096]{1,0:T(8,128)(2,1)}, bf16[128,4096]{1,0:T(8,128)(2,1)}), (bf16[128,4096]{1,0:T(8,128)(2,1)}, bf16[128,4096]{1,0:T(8,128)(2,1)})) %all-reduce.21.cloned.1.call-update) | async-done | bytes 2097168
  875.3 27.0 %all-gather.27.cloned.1.call-done = bf16[8,128,7,128]{3,1,0,2:T(8,128)(2,1)} async-done(((bf16[2,128,7,128]{3,1,0,2:T(8,128)(2,1)}), bf16[8,128,7,128]{3,1,0,2:T(8,128)(2,1)}) %all-gather.27.cloned.1.call-update) | async-done | bytes 1835024 | tf_op jit(solution)/shard_map/all_gather | solution.py:168
  902.2 2.8 fusion.119
  905.0 27.5 %all-gather.25.cloned.1.call-done = bf16[8,128,7,128]{3,1,0,2:T(8,128)(2,1)} async-done(((bf16[2,128,7,128]{3,1,0,2:T(8,128)(2,1)}), bf16[8,128,7,128]{3,1,0,2:T(8,128)(2,1)}) %all-gather.25.cloned.1.call-update) | async-done | bytes 1835024 | tf_op jit(solution)/shard_map/all_gather | solution.py:167
  932.5 2.7 fusion.118
  935.2 82.0 %all-gather.23.cloned.1.call-done = bf16[8,128,4096]{2,1,0:T(8,128)(2,1)} async-done(((bf16[2,128,4096]{2,1,0:T(8,128)(2,1)}), bf16[8,128,4096]{2,1,0:T(8,128)(2,1)}) %all-gather.23.cloned.1.call-update) | async-done | bytes 8388624 | tf_op jit(solution)/shard_map/all_gather | solution.py:165
  1017.2 5.7 fusion.116
  1027.1 2.2 copy.268
  1029.3 1.9 constant_dynamic-slice_fusion.7
  1031.3 2.9 copy.259
  1037.8 2.1 copy.266
  1039.9 1.9 constant_dynamic-slice_fusion.8
  1041.8 2.8 copy.258
  1048.4 2.1 copy.264
  1052.5 3.0 copy.257
  1059.2 2.7 convolution_bitcast_fusion.4
  1073.2 29.7 %all-gather.29.cloned.1.call-done = bf16[8,128,4096]{2,1,0:T(8,128)(2,1)} async-done(((bf16[2,128,4096]{2,1,0:T(8,128)(2,1)}), bf16[8,128,4096]{2,1,0:T(8,128)(2,1)}) %all-gather.29.cloned.1.call-update) | async-done | bytes 8388624 | tf_op jit(solution)/shard_map/all_gather | solution.py:169
  1103.0 5.2 fusion.117
  1110.0 2.1 copy.207
  1112.1 5.7 gather_fusion.11
  1117.8 7.5 gather_fusion.8
  1126.6 5.9 gather_fusion.5
  1132.6 2.1 copy.265
  1135.5 5.7 gather_fusion.2
  1141.2 3.8 convolution_bitcast_fusion
  1145.0 3.8 convolution_bitcast_fusion.1
  1148.9 2.1 convolution_bitcast_fusion.2
  1151.1 2.1 convolution_bitcast_fusion.3
  1154.8 2.6 add_convert_fusion
  (356 shorter events, 138.8 us)
Async XLA Ops:
  7.2 88.2 %all-gather.13.cloned.1.call-start = ((), (), s32[]{:S(2)}) async-start(), calls=%async_computation | async-start | bytes 1114112 | tf_op jit(solution)/shard_map/all_gather | solution.py:83
  9.8 187.5 %all-reduce.13.cloned.1.call-start = ((), (), s32[]{:S(2)}) async-start(), calls=%async_computation.11 | async-start | bytes 2097152
  77.6 4.3 copy-start.12
  95.4 12.3 %copy-start.72 = (u32[128]{0:T(128)S(1)}, u32[128]{0:T(128)}, u32[]{:S(2)}) copy-start(u32[128]{0:T(128)} %constant.279) | copy-start | bytes 1540
  95.4 6.0 copy-start
  95.4 6.0 copy-start.26
  101.4 3.1 copy-start.3
  106.6 94.9 %copy-start.60 = (f32[1,4096]{1,0:T(1,128)S(1)}, f32[1,4096]{1,0:T(1,128)}, u32[]{:S(2)}) copy-start(f32[1,4096]{1,0:T(1,128)} %param.20) | copy-start | bytes 49156
  107.6 136.8 %all-gather.15.cloned.1.call-start = ((), (), s32[]{:S(2)}) async-start(), calls=%async_computation.1 | async-start | bytes 1114112 | tf_op jit(solution)/shard_map/all_gather | solution.py:83
  198.3 2.2 collective-permute-start
  202.2 142.9 %all-reduce.15.cloned.1.call-start = ((), (), s32[]{:S(2)}) async-start(), calls=%async_computation.12 | async-start | bytes 2097152
  244.4 103.8 %copy-start.61 = (bf16[2,8,4096]{2,1,0:T(8,128)(2,1)S(1)}, bf16[2,8,4096]{2,1,0:T(8,128)(2,1)}, u32[]{:S(2)}) copy-start(bf16[2,8,4096]{2,1,0:T(8,128)(2,1)} %param.18) | copy-start | bytes 393220
  244.4 6.0 copy-start.1
  244.5 6.0 copy-start.22
  250.4 2.5 copy-start.58
  250.5 3.2 copy-start.4
  257.7 94.2 %copy-start.56 = (f32[128,7,128]{2,0,1:T(8,128)}, f32[128,7,128]{2,0,1:T(8,128)S(1)}, u32[]{:S(2)}) copy-start(f32[128,7,128]{2,0,1:T(8,128)S(1)} %get-tuple-element.357) | copy-start | bytes 1376260
  257.7 91.6 %copy-start.66 = (bf16[2,8,4096]{2,1,0:T(8,128)(2,1)S(1)}, bf16[2,8,4096]{2,1,0:T(8,128)(2,1)}, u32[]{:S(2)}) copy-start(bf16[2,8,4096]{2,1,0:T(8,128)(2,1)} %param.19) | copy-start | bytes 393220
  258.6 132.7 %all-gather.17.cloned.1.call-start = ((), (), s32[]{:S(2)}) async-start(), calls=%async_computation.2 | async-start | bytes 1114112 | tf_op jit(solution)/shard_map/all_gather | solution.py:83
  346.0 7.9 copy-start.62
  346.1 2.2 collective-permute-start.1
  348.3 5.6 copy-start.55
  349.2 86.3 %all-gather.33.cloned.1.call-start = ((), (), s32[]{:S(2)}) async-start(), calls=%async_computation.10 | async-start | bytes 1114112 | tf_op jit(solution)/shard_map/all_gather | solution.py:135
  349.9 192.1 %all-reduce.17.cloned.1.call-start = ((), (), s32[]{:S(2)}) async-start(), calls=%async_computation.13 | async-start | bytes 2097152
  353.9 4.8 copy-start.57
  393.1 42.4 %copy-start.42 = (bf16[128,4096]{1,0:T(8,128)(2,1)}, bf16[128,4096]{1,0:T(8,128)(2,1)S(1)}, u32[]{:S(2)}) copy-start(bf16[128,4096]{1,0:T(8,128)(2,1)S(1)} %get-tuple-element.239) | copy-start | bytes 3145732
  438.3 153.2 %all-gather.19.cloned.1.call-start = ((), (), s32[]{:S(2)}) async-start(), calls=%async_computation.3 | async-start | bytes 1114112 | tf_op jit(solution)/shard_map/all_gather | solution.py:135
  544.7 3.1 collective-permute-start.2
  549.3 150.2 %all-reduce.19.cloned.1.call-start = ((), (), s32[]{:S(2)}) async-start(), calls=%async_computation.14 | async-start | bytes 2097152
  591.5 109.0 %copy-start.64 = (bf16[8,4096]{1,0:T(8,128)(2,1)S(1)}, bf16[8,4096]{1,0:T(8,128)(2,1)}, u32[]{:S(2)}) copy-start(bf16[8,4096]{1,0:T(8,128)(2,1)} %bitcast_select_fusion.14) | copy-start | bytes 196612
  597.4 2.5 copy-start.17
  603.4 7.2 slice-start.2
  605.6 5.0 slice-start.3
  605.6 5.0 copy-start.18
  605.6 5.0 copy-start.28
  613.0 135.3 %all-gather.21.cloned.1.call-start = ((), (), s32[]{:S(2)}) async-start(), calls=%async_computation.4 | async-start | bytes 1114112 | tf_op jit(solution)/shard_map/all_gather | solution.py:135
  701.5 3.1 collective-permute-start.3
  706.2 85.3 %all-gather.31.cloned.1.call-start = ((), (), s32[]{:S(2)}) async-start(), calls=%async_computation.9 | async-start | bytes 2293760 | tf_op jit(solution)/shard_map/all_gather | solution.py:166
  709.2 163.2 %all-reduce.21.cloned.1.call-start = ((), (), s32[]{:S(2)}) async-start(), calls=%async_computation.15 | async-start | bytes 4194304
  754.2 2.5 copy-start.19
  760.2 7.2 slice-start.4
  762.4 5.0 slice-start.5
  762.4 5.1 copy-start.20
  762.4 5.1 copy-start.29
  769.9 132.4 %all-gather.27.cloned.1.call-start = ((), (), s32[]{:S(2)}) async-start(), calls=%async_computation.7 | async-start | bytes 2293760 | tf_op jit(solution)/shard_map/all_gather | solution.py:168
  774.0 158.5 %all-gather.25.cloned.1.call-start = ((), (), s32[]{:S(2)}) async-start(), calls=%async_computation.6 | async-start | bytes 2293760 | tf_op jit(solution)/shard_map/all_gather | solution.py:167
  777.9 5.5 copy-start.21
  783.3 234.0 %all-gather.23.cloned.1.call-start = ((), (), s32[]{:S(2)}) async-start(), calls=%async_computation.5 | async-start | bytes 10485760 | tf_op jit(solution)/shard_map/all_gather | solution.py:165
  786.3 316.7 %all-gather.29.cloned.1.call-start = ((), (), s32[]{:S(2)}) async-start(), calls=%async_computation.8 | async-start | bytes 10485760 | tf_op jit(solution)/shard_map/all_gather | solution.py:169
  797.1 77.1 %copy-start.65 = (bf16[8,4096]{1,0:T(8,128)(2,1)S(1)}, bf16[8,4096]{1,0:T(8,128)(2,1)}, u32[]{:S(2)}) copy-start(bf16[8,4096]{1,0:T(8,128)(2,1)} %bitcast_select_fusion.12) | copy-start | bytes 196612
  874.2 61.0 %copy-start.67 = (bf16[1,2,8,4096]{3,2,1,0:T(8,128)(2,1)}, bf16[1,2,8,4096]{3,2,1,0:T(8,128)(2,1)S(1)}, u32[]{:S(2)}) copy-start(bf16[1,2,8,4096]{3,2,1,0:T(8,128)(2,1)S(1)} %fusion.99) | copy-start | bytes 393220
  875.2 60.0 %copy-start.68 = (bf16[1,2,8,4096]{3,2,1,0:T(8,128)(2,1)}, bf16[1,2,8,4096]{3,2,1,0:T(8,128)(2,1)S(1)}, u32[]{:S(2)}) copy-start(bf16[1,2,8,4096]{3,2,1,0:T(8,128)(2,1)S(1)} %fusion.102) | copy-start | bytes 393220
  1059.2 2.7 copy-start.51
  1062.4 2.6 copy-start.6
  1062.4 2.6 copy-start.50
  1117.8 7.5 copy-start.30
  1141.2 7.7 slice-start.6
  1145.0 3.9 slice-start.7
  1145.0 5.9 slice-start.8
  1151.0 2.6 copy-start.34
  1151.0 3.0 copy-start.35
  1151.0 3.4 copy-start.36
  1151.0 3.8 copy-start.37
  1151.1 3.8 copy-start.69
  (28 other events, 44.3 us)
Sparse Core Ops, SparseCore 0:
  10.7 45.3 all-gather.12
  107.7 89.5 all-reduce.12
  202.4 42.0 all-gather.14
  258.8 86.3 all-reduce.14
  349.3 42.0 all-gather.16
  393.4 42.0 all-gather.32
  438.8 103.2 all-reduce.16
  549.5 41.9 all-gather.18
  613.1 86.3 all-reduce.18
  706.3 41.9 all-gather.20
  750.0 27.8 all-gather.30
  781.7 90.5 all-reduce.20
  874.1 28.0 all-gather.26
  903.8 28.6 all-gather.24
  934.1 83.0 all-gather.22
  1018.9 84.0 all-gather.28
where the time goes:
time: 1170 us; the launch traced here: 1160 us
  waiting for transfers between devices  801 us (68%)
  local copies, waits for them, and re-layouts  195 us (17%)
  matrix products  89.3 us (8%)
  other arithmetic  55.2 us (5%)
  between operations  16.2 us (1%)
    unnamed x21, waiting for transfers between devices  435 us
    all_gather x3, waiting for transfers between devices, shards(): grad_full = lax.all_gather(delta, 'ts', axis=0, tiled=True)  122 us
    all_gather x1, waiting for transfers between devices, shards(): normed_all = lax.all_gather(normed_store, 'dp', axis=0, tiled=True)  82 us
    all_gather x3, waiting for transfers between devices, shards(): gathered = lax.all_gather(normed, 'ts', axis=0, tiled=True)  72.8 us
    unnamed x128, local copies, waits for them, and re-layouts  46.4 us
    all_gather x1, waiting for transfers between devices, shards(): delta_all = lax.all_gather(delta_store, 'dp', axis=0, tiled=True)  29.7 us
    all_gather x1, waiting for transfers between devices, shards(): dgate_all = lax.all_gather(dgate_store, 'dp', axis=0, tiled=True)  27.5 us
    all_gather x1, waiting for transfers between devices, shards(): dup_all = lax.all_gather(dup_store, 'dp', axis=0, tiled=True)  27 us
  transfers between devices with their start and end apart: 20, of which 18 were waited for; matrix products, arithmetic and copies ran while one was open for 18% of the time, Pallas kernels for 0%

commit v1 on v0

v1 whole, which is shorter than its diff:
```python
import functools
import math

import jax
import jax.numpy as jnp
from jax import lax
from jax.experimental import pallas as pl
from jax.experimental.pallas import tpu as pltpu
from jax.sharding import PartitionSpec as P

EPSILON = 1e-05
MESH = pl.DeviceIdType.MESH
F32 = jnp.float32
BF16 = jnp.bfloat16
NT = (((1,), (1,)), ((), ()))


def kernel(
    side, n_dp,
    x_ref, cot_ref, gain_ref, w_hbm, inv_ref, rows_ref, live_ref,
    seg_ref, ing_ref, wg_ref,
    raw0, raw1, raw2, wgu, wd, g, part, rs1, rs2, mid, hop, gu, dhid, hid, hid_t, dgu, xt, db, ex1, ex2,
    w_sem, ag_send, ag_recv, rs_send, rs_recv, hop_send, hop_recv, ex_send, ex_recv,
):
    rows, width = x_ref.shape
    half = width // 2
    _, hb, slots, block, _ = w_hbm.shape
    kb = width // block
    tokens = side * side * rows
    quarter = block // n_dp
    sec = lax.axis_index("section")
    ts = lax.axis_index("ts")
    me = lax.axis_index("dp")
    z, y = ts // side, lax.rem(ts, side)
    right, left = lax.rem(me + 1, n_dp), lax.rem(me + n_dp - 1, n_dp)
    across = lax.rem(me + 2, n_dp)
    raw = (raw0, raw1, raw2)
    cols = (slice(0, half), slice(half, width))
    peers = [
        (lax.rem(z + d, side), lax.rem(y + d, side)) for d in range(1, side)
    ]

    w_copies = [
        pltpu.make_async_copy(w_hbm.at[m], raw[m].at[:, pl.ds(0, slots)], w_sem.at[m])
        for m in range(3)
    ]
    for copy in w_copies:
        copy.start()

    barrier = pltpu.get_barrier_semaphore()
    for pz, py in peers:
        pl.semaphore_signal(barrier, inc=1, device_id={"ts": pz * side + y}, device_id_type=MESH)
        pl.semaphore_signal(barrier, inc=1, device_id={"ts": z * side + py}, device_id_type=MESH)
    pl.semaphore_signal(barrier, inc=1, device_id={"dp": right}, device_id_type=MESH)
    pl.semaphore_signal(barrier, inc=1, device_id={"dp": left}, device_id_type=MESH)
    pl.semaphore_signal(barrier, inc=1, device_id={"section": 1 - sec}, device_id_type=MESH)
    pl.semaphore_wait(barrier, 2 * (side - 1) + 3)

    def remote(src, dst, send, recv, where):
        return pltpu.make_async_remote_copy(
            src_ref=src, dst_ref=dst, send_sem=send, recv_sem=recv,
            device_id=where, device_id_type=MESH,
        )

    def gather_copies(i, phase, part_of):
        copies = []
        for d, (pz, py) in enumerate(peers):
            if phase == 0:
                ref = g.at[i, z, y, :, cols[part_of]]
            elif part_of == 0:
                ref = g.at[i, z, :, :, cols[0]]
            else:
                ref = g.at[i, :, y, :, cols[1]]
            along_y = phase == part_of
            where = {"ts": z * side + py} if along_y else {"ts": pz * side + y}
            at = phase * 2 + part_of
            copies.append(remote(ref, ref, ag_send.at[i, at, d], ag_recv.at[i, at, d], where))
        return copies

    def gather_first(i):
        for part_of in (0, 1):
            for copy in gather_copies(i, 0, part_of):
                copy.start()

    def gather_second(i):
        for part_of in (0, 1):
            for copy in gather_copies(i, 0, part_of):
                copy.wait_recv()
            for copy in gather_copies(i, 1, part_of):
                copy.start()

    def gather_end(i):
        for part_of in (0, 1):
            for copy in gather_copies(i, 1, part_of):
                copy.wait_recv()
        for phase in (0, 1):
            for part_of in (0, 1):
                for copy in gather_copies(i, phase, part_of):
                    copy.wait_send()

    def scatter_copies(use, phase, part_of):
        copies = []
        for d, (pz, py) in enumerate(peers):
            if phase == 0 and part_of == 0:
                src, where = part.at[pz, :, :, cols[0]], {"ts": pz * side + y}
            elif phase == 0:
                src, where = part.at[:, py, :, cols[1]], {"ts": z * side + py}
            elif part_of == 0:
                src, where = mid.at[0, py], {"ts": z * side + py}
            else:
                src, where = mid.at[1, pz], {"ts": pz * side + y}
            dst = (rs1 if phase == 0 else rs2).at[use, part_of, d]
            at = phase * 2 + part_of
            copies.append(remote(src, dst, rs_send.at[use, at, d], rs_recv.at[use, at, d], where))
        return copies

    def scatter_start(use, part_of):
        for copy in scatter_copies(use, 0, part_of):
            copy.start()

    def scatter_middle(use):
        for part_of in (0, 1):
            for copy in scatter_copies(use, 0, part_of):
                copy.wait_recv()
            for i in range(side):
                own = part[z, i, :, cols[0]] if part_of == 0 else part[i, y, :, cols[1]]
                total = own.astype(F32)
                for d in range(side - 1):
                    total = total + rs1[use, part_of, d, i].astype(F32)
                mid[part_of, i] = total.astype(BF16)
            for copy in scatter_copies(use, 1, part_of):
                copy.start()

    def scatter_end(use):
        totals = []
        for part_of in (0, 1):
            for copy in scatter_copies(use, 1, part_of):
                copy.wait_recv()
            total = mid[part_of, y if part_of == 0 else z].astype(F32)
            for d in range(side - 1):
                total = total + rs2[use, part_of, d].astype(F32)
            totals.append(total)
        for phase in (0, 1):
            for part_of in (0, 1):
                for copy in scatter_copies(use, phase, part_of):
                    copy.wait_send()
        return jnp.concatenate(totals, axis=1)

    def scale_of(values):
        return lax.rsqrt(jnp.mean(values * values, axis=-1, keepdims=True) + EPSILON)

    def normed_of(values):
        return (values * scale_of(values) * gain_ref[...]).astype(BF16)

    def flat(i):
        return g[i].reshape(tokens, width)

    def section_copy(src):
        return remote(src, hop, hop_send, hop_recv, {"section": 1 - sec})

    @pl.when(sec == 0)
    def _():
        g[0, z, y] = normed_of(x_ref[...].astype(F32))

    @pl.when(sec == 1)
    def _():
        g[0, z, y] = cot_ref[...]

    gather_first(0)

    for m in range(3):
        raw[m][:, slots] = jnp.zeros((hb, block, block), BF16)
    wd[hb * block:] = jnp.zeros((wd.shape[0] - hb * block, width), BF16)
    w_copies[0].wait()
    w_copies[1].wait()

    @pl.loop(0, kb)
    def _(k):
        for m in range(2):
            for c in range(hb):
                slot = inv_ref[(m * hb + c) * kb + k]
                at = (2 * c + m) * block
                wgu[pl.ds(k * block, block), at : at + block] = raw[m][c, slot]

    gather_second(0)
    w_copies[2].wait()

    @pl.loop(0, kb)
    def _(k):
        column = pl.ds(pl.multiple_of(k * block, block), block)
        for c in range(hb):
            slot = inv_ref[(2 * hb + c) * kb + k]
            wd[c * block : (c + 1) * block, column] = raw[2][c, slot]

    gather_end(0)

    def down_grad_input(i):
        @pl.loop(0, wd.shape[0] // (2 * block))
        def _(p):
            at = pl.multiple_of(p * 2 * block, 2 * block)
            dhid[:, pl.ds(at, 2 * block)] = lax.dot_general(
                flat(i), wd[pl.ds(at, 2 * block), :], NT, preferred_element_type=F32
            )

    @pl.when(sec == 1)
    def _():
        down_grad_input(0)
        section_copy(seg_ref).wait_recv()
        g[1, z, y] = normed_of(hop[...].astype(F32))
        gather_first(1)
        gather_second(1)
        gather_end(1)

    @pl.loop(0, hb)
    def _(c):
        both = jnp.dot(
            flat(sec), wgu[:, pl.ds(pl.multiple_of(c * 2 * block, 2 * block), 2 * block)],
            preferred_element_type=F32,
        )
        gu[c] = both
        gate, upper = both[:, :block], both[:, block:]
        hidden = (gate * jax.nn.sigmoid(gate) * upper).astype(BF16)
        hid[:, pl.ds(pl.multiple_of(c * block, block), block)] = hidden

    def transposes():
        @pl.loop(0, kb)
        def _(k):
            column = pl.ds(pl.multiple_of(k * block, block), block)
            xt[k] = g[sec, :, :, :, column].reshape(tokens, block).T

        @pl.loop(0, hb)
        def _(c):
            hid_t[c] = hid[:, pl.ds(pl.multiple_of(c * block, block), block)].T

    def delta_blocks():
        @pl.loop(0, kb)
        def _(k):
            column = pl.ds(pl.multiple_of(k * block, block), block)
            db[k] = g[1 - sec, :, :, :, column].reshape(tokens, block)

    tile = min(512, half)

    def down(use):
        for part_of in (0, 1):
            @pl.loop(0, half // tile)
            def _(n):
                at = pl.multiple_of(part_of * half + n * tile, tile)
                out = jnp.dot(hid[...], wd[: hb * block, pl.ds(at, tile)], preferred_element_type=F32)
                part[:, :, :, pl.ds(at, tile)] = out.astype(BF16).reshape(side, side, rows, tile)
            scatter_start(use, part_of)

    def back(use):
        for part_of in (0, 1):
            @pl.loop(0, half // tile)
            def _(n):
                at = pl.multiple_of(part_of * half + n * tile, tile)
                out = lax.dot_general(
                    dgu[...], wgu[pl.ds(at, tile), :], NT, preferred_element_type=F32
                )
                part[:, :, :, pl.ds(at, tile)] = out.astype(BF16).reshape(side, side, rows, tile)
            scatter_start(use, part_of)

    def input_grad(values, delta, d_norm):
        scale = scale_of(values)
        scaled = gain_ref[...] * d_norm
        spread = jnp.mean(scaled * values, axis=-1, keepdims=True)
        return (delta + scale * scaled - values * (scale * scale * scale) * spread).astype(BF16)

    @pl.when(sec == 0)
    def _():
        down(0)
        scatter_middle(0)
        seg_ref[...] = (x_ref[...].astype(F32) + scatter_end(0)).astype(BF16)
        sent = section_copy(seg_ref)
        sent.start()
        transposes()
        sent.wait_send()
        sent.wait_recv()
        g[1, z, y] = hop[...]
        gather_first(1)
        gather_second(1)
        gather_end(1)
        down_grad_input(1)

    @pl.loop(0, hb)
    def _(c):
        gate, upper = gu[c, :, :block], gu[c, :, block:]
        d_hidden = dhid[:, pl.ds(pl.multiple_of(c * block, block), block)]
        sig = jax.nn.sigmoid(gate)
        d_gate = d_hidden * upper * sig * (1.0 + gate * (1.0 - sig))
        d_up = d_hidden * gate * sig
        at = pl.multiple_of(c * 2 * block, 2 * block)
        dgu[:, pl.ds(at, block)] = d_gate.astype(BF16)
        dgu[:, pl.ds(pl.multiple_of(at + block, block), block)] = d_up.astype(BF16)

    @pl.when(sec == 1)
    def _():
        back(0)
        transposes()
        scatter_middle(0)
        ing_ref[...] = input_grad(hop[...].astype(F32), cot_ref[...].astype(F32), scatter_end(0))
        section_copy(ing_ref).start()

    delta_blocks()
    first, second = slice(0, slots // 2), slice(slots // 2, slots)

    def quarter_of(q):
        return pl.ds(pl.multiple_of(q * quarter, quarter), quarter)

    def ring_first(m, c):
        i = m * hb + c
        q = quarter_of(across)
        return (
            remote(raw[m].at[c, first, q], ex1.at[0, m, c], ex_send.at[0, 0, i], ex_recv.at[0, 0, i], {"dp": right}),
            remote(raw[m].at[c, second, q], ex1.at[1, m, c], ex_send.at[0, 1, i], ex_recv.at[0, 1, i], {"dp": left}),
        )

    def ring_second(m, c):
        i = m * hb + c
        here = pl.ds(0, slots)
        return (
            remote(raw[m].at[c, here, quarter_of(right)], ex2.at[0, m, c], ex_send.at[1, 0, i], ex_recv.at[1, 0, i], {"dp": right}),
            remote(raw[m].at[c, here, quarter_of(left)], ex2.at[1, m, c], ex_send.at[1, 1, i], ex_recv.at[1, 1, i], {"dp": left}),
        )

    def pass_on(m, c):
        for copy, into, which, arrived in zip(ring_first(m, c), (right, left), (first, second), (0, 1)):
            copy.wait_recv()
            q = quarter_of(into)
            mine = raw[m][c, which, q, :].astype(F32)
            raw[m][c, which, q, :] = (mine + ex1[arrived, m, c].astype(F32)).astype(BF16)
        for copy in ring_second(m, c):
            copy.start()

    def live_of(m, c, j):
        return live_ref[(m * hb + c) * slots + j].astype(F32)

    @pl.loop(0, hb)
    def _(c):
        picked = []
        for j in range(slots):
            picked.append(db[rows_ref[(2 * hb + c) * slots + j]])
        out = jnp.dot(hid_t[c], jnp.concatenate(picked, axis=1), preferred_element_type=F32)
        for j in range(slots):
            raw[2][c, j] = (out[:, j * block : (j + 1) * block] * live_of(2, c, j)).astype(BF16)
        for copy in ring_first(2, c):
            copy.start()

    for m in range(2):
        @pl.loop(0, hb)
        def _(c):
            at = pl.multiple_of((2 * c + m) * block, block)
            d_block = dgu[:, pl.ds(at, block)]
            picked = [xt[rows_ref[(m * hb + c) * slots + j]] for j in range(slots)]
            out = jnp.dot(jnp.concatenate(picked, axis=0), d_block, preferred_element_type=F32)
            for j in range(slots):
                raw[m][c, j] = (out[j * block : (j + 1) * block] * live_of(m, c, j)).astype(BF16)
            for copy in ring_first(m, c):
                copy.start()
            pass_on((m + 2) % 3, c)

    @pl.loop(0, hb)
    def _(c):
        pass_on(1, c)

    @pl.when(sec == 0)
    def _():
        back(1)
        scatter_middle(1)
        ing_ref[...] = input_grad(x_ref[...].astype(F32), hop[...].astype(F32), scatter_end(1))

    @pl.when(sec == 1)
    def _():
        section_copy(ing_ref).wait_send()
        down(1)
        scatter_middle(1)
        seg_ref[...] = (hop[...].astype(F32) + scatter_end(1)).astype(BF16)

    for m in (2, 0, 1):
        @pl.loop(0, hb)
        def _(c):
            for copy in ring_second(m, c):
                copy.wait_recv()
            total = raw[m][c, pl.ds(0, slots), quarter_of(me), :].astype(F32)
            for way in (0, 1):
                total = total + ex2[way, m, c].astype(F32)
            wg_ref[m, c] = total.astype(BF16)
            for copy in ring_first(m, c) + ring_second(m, c):
                copy.wait_send()


def shards(inputs, cotangent, gains, weights, block_rows, block_count):
    n_dp, n_ts = lax.axis_size("dp"), lax.axis_size("ts")
    side = math.isqrt(n_ts)
    micro, shard_rows, width = inputs.shape
    rows = micro * shard_rows
    _, _, hb, slots, block, _ = weights.shape
    kb = width // block
    half = width // 2
    quarter = block // n_dp
    tokens = rows * n_ts
    lists = block_rows[0]
    live = jnp.arange(slots)[None, None, :] < block_count[0][:, :, None]
    match = (lists[..., None] == jnp.arange(kb)) & live[..., None]
    inverse = jnp.min(jnp.where(match, jnp.arange(slots)[:, None], slots), axis=2)
    vmem = pl.BlockSpec(memory_space=pltpu.VMEM)
    smem = pl.BlockSpec(memory_space=pltpu.SMEM)
    hb2 = (hb + 1) // 2 * 2
    seg, ing, wg = pl.pallas_call(
        functools.partial(kernel, side, n_dp),
        out_shape=(
            jax.ShapeDtypeStruct((rows, width), BF16),
            jax.ShapeDtypeStruct((rows, width), BF16),
            jax.ShapeDtypeStruct((3, hb, slots, quarter, block), BF16),
        ),
        in_specs=[vmem, vmem, vmem, pl.BlockSpec(memory_space=pl.ANY), smem, smem, smem],
        out_specs=(vmem, vmem, vmem),
        scratch_shapes=[
            pltpu.VMEM((hb, slots + 1, block, block), BF16),
            pltpu.VMEM((hb, slots + 1, block, block), BF16),
            pltpu.VMEM((hb, slots + 1, block, block), BF16),
            pltpu.VMEM((width, 2 * hb * block), BF16),
            pltpu.VMEM((hb2 * block, width), BF16),
            pltpu.VMEM((2, side, side, rows, width), BF16),
            pltpu.VMEM((side, side, rows, width), BF16),
            pltpu.VMEM((2, 2, side - 1, side, rows, half), BF16),
            pltpu.VMEM((2, 2, side - 1, rows, half), BF16),
            pltpu.VMEM((2, side, rows, half), BF16),
            pltpu.VMEM((rows, width), BF16),
            pltpu.VMEM((hb, tokens, 2 * block), F32),
            pltpu.VMEM((tokens, hb2 * block), F32),
            pltpu.VMEM((tokens, hb * block), BF16),
            pltpu.VMEM((hb, block, tokens), BF16),
            pltpu.VMEM((tokens, 2 * hb * block), BF16),
            pltpu.VMEM((kb, block, tokens), BF16),
            pltpu.VMEM((kb, tokens, block), BF16),
            pltpu.VMEM((2, 3, hb, slots // 2, quarter, block), BF16),
            pltpu.VMEM((2, 3, hb, slots, quarter, block), BF16),
            pltpu.SemaphoreType.DMA((3,)),
            pltpu.SemaphoreType.DMA((2, 4, side - 1)),
            pltpu.SemaphoreType.DMA((2, 4, side - 1)),
            pltpu.SemaphoreType.DMA((2, 4, side - 1)),
            pltpu.SemaphoreType.DMA((2, 4, side - 1)),
            pltpu.SemaphoreType.DMA,
            pltpu.SemaphoreType.DMA,
            pltpu.SemaphoreType.DMA((2, 2, 3 * hb)),
            pltpu.SemaphoreType.DMA((2, 2, 3 * hb)),
        ],
        compiler_params=pltpu.CompilerParams(
            collective_id=0, has_side_effects=True, vmem_limit_bytes=63 * 1024 * 1024
        ),
    )(
        inputs.reshape(rows, width),
        cotangent.reshape(rows, width),
        gains,
        weights[0],
        inverse.reshape(-1).astype(jnp.int32),
        lists.reshape(-1),
        live.reshape(-1).astype(jnp.int32),
    )
    shape = (1, micro, shard_rows, width)
    return seg.reshape(shape), ing.reshape(shape), wg[None]


def solution(mesh):
    in_specs = (
        P(None, ("dp", "ts"), None),
        P(None, ("dp", "ts"), None),
        P("section", None),
        P("section", None, "ts", None, None, None),
        P("section", None, "ts", None),
        P("section", None, "ts"),
    )
    out_specs = (
        P("section", None, ("dp", "ts"), None),
        P("section", None, ("dp", "ts"), None),
        P("section", None, "ts", None, "dp", None),
    )
    return jax.shard_map(shards, mesh=mesh, in_specs=in_specs, out_specs=out_specs, check_vma=False)
```

time: 1170 us -> 183 us (0.16)
  waiting for transfers between devices: 801 us -> 0 us
  local copies, waits for them, and re-layouts: 195 us -> 10.1 us
  Pallas kernels: 0 us -> 171 us
  matrix products: 89.3 us -> 0 us
  other arithmetic: 55.2 us -> 0.95 us
  between operations: 16.2 us -> 0.65 us
    unnamed x21 -> x0, waiting for transfers between devices: 435 us -> none
    all_gather x11 -> x0, waiting for transfers between devices: 361 us -> none  [the longest x3 122 us: shards(): grad_full = lax.all_gather(delta, 'ts', axis=0, tiled=True)]
    pallas_call x0 -> x1, Pallas kernels: none -> 171 us  [shards(): pl.pallas_call(functools.partial(kernel, side, n_dp), out_shape=(jax.Shap...]
    dot_general x27 -> x0, matrix products: 89.3 us -> none  [the longest x2 12 us: ffn_forward(): upper = jnp.dot(gathered, placed_up, preferred_element_type=jnp.float32)]
    unnamed x128 -> x4, local copies, waits for them, and re-layouts: 46.4 us -> 7.21 us
    gather x12 -> x0, local copies, waits for them, and re-layouts: 37.4 us -> none  [the longest x4 24.9 us: shards(): delta_all[low_row:high_row].reshape(-1, row_blocks, block)[:, lists[2]]]
    convert_element_type x2 -> x1, local copies, waits for them, and re-layouts: 25.9 us -> 0.66 us  [shards(): live.reshape(-1).astype(jnp.int32)]
    slice x9 -> x0, local copies, waits for them, and re-layouts: 21.6 us -> none  [the longest x1 5.67 us: shards(): feats = normed_all[low_row:high_row].reshape(-1, row_blocks, block)]
  transfers between devices with their start and end apart: 20 -> 0, of which waited for: 18 -> 0; matrix products, arithmetic and copies ran while one was open for 18% -> 0% of each run, Pallas kernels for 0% -> 0%
where the time goes in v1:
time: 183 us; the launch traced here: 182 us
  Pallas kernels  171 us (93%)
  local copies, waits for them, and re-layouts  10.1 us (6%)
    pallas_call x1, Pallas kernels, shards(): pl.pallas_call(functools.partial(kernel, side, n_dp), out_shape=(jax.Shap...  171 us
    unnamed x4, local copies, waits for them, and re-layouts  7.21 us

profile of v1, /device:TPU:0, one launch (start us, length us, event | category | flops | bytes accessed | tf_op | source)
XLA Modules:
  0.0 182.3 jit_solution(9384044639375036323)
XLA Ops:
  0.6 0.7 copy.15
  1.3 0.7 reduce
  2.1 0.7 reshape_squeeze.3.rows_ref
  2.7 0.1 fusion.1
  2.8 0.7 reshape.37.live_ref
  3.4 0.1 copy.11
  3.6 0.8 copy.12
  4.4 0.1 select_reduce_fusion
  4.5 0.7 reshape.34.inv_ref
  5.2 170.5 %shard_map.85 = (bf16[16,4096]{1,0:T(8,128)(2,1)}, bf16[16,4096]{1,0:T(8,128)(2,1)}, bf16[3,7,12,32,128]{4,3,2,1,0:T(8,128)(2,1)}) custom-call(bf16[16,4096]{1,0:T(8,128)(2,1)} %bitcast.12, bf16[16,4096]{1,0:T(8,128)(2,1)} %bitcast.13, f32[1,4096]{1,0:T(1,128)} %gain_ref.1, bf16[3,7,12,128,128]{4,3,2,1,0:T(8,128)(2,1)} %bitcast.10, s32[672]{0:T(1024)} %reshape.34.inv_ref, ...), custom_call_target="tpu_custom_call" | custom-call | tf_op jit(solution)/shard_map/pallas_call | solution.py:409
  175.7 1.6 copy.19
  177.3 1.6 copy.20
  178.9 3.4 %copy.21 = bf16[1,3,7,12,32,128]{5,4,3,2,1,0:T(8,128)(2,1)} copy(bf16[1,3,7,12,32,128]{5,4,3,2,1,0:T(8,128)(2,1)} %bitcast.11) | data formatting | bytes 4128768

commit v2 on v1

v2 whole, which is shorter than its diff:
```python
import functools
import math

import jax
import jax.numpy as jnp
from jax import lax
from jax.experimental import pallas as pl
from jax.experimental.pallas import tpu as pltpu
from jax.sharding import PartitionSpec as P

EPSILON = 1e-05
MESH = pl.DeviceIdType.MESH
F32 = jnp.float32
BF16 = jnp.bfloat16
NT = (((1,), (1,)), ((), ()))


def kernel(
    side, n_dp,
    x_ref, cot_ref, gain_ref, w_hbm, inv_ref, rows_ref, live_ref,
    seg_ref, ing_ref, wg_ref,
    raw0, raw1, raw2, wgu, wd, g, part, rs1, rs2, mid, hop, stage, gain_x, gu, dhid, hid, hid_t, dgu, xt, db, ex1, ex2,
    w_sem, ag_send, ag_recv, rs_send, rs_recv, hop_send, hop_recv, ex_send, ex_recv,
):
    rows, width = x_ref.shape
    chunk = width // 4
    _, hb, slots, block, _ = w_hbm.shape
    kb = width // block
    tokens = side * side * rows
    quarter = block // n_dp
    sec = lax.axis_index("section")
    ts = lax.axis_index("ts")
    me = lax.axis_index("dp")
    z, y = ts // side, lax.rem(ts, side)
    right, left = lax.rem(me + 1, n_dp), lax.rem(me + n_dp - 1, n_dp)
    across = lax.rem(me + 2, n_dp)
    raw = (raw0, raw1, raw2)
    cols = [slice(q * chunk, (q + 1) * chunk) for q in range(4)]
    order = (0, 2, 1, 3)
    peers = [(lax.rem(z + d, side), lax.rem(y + d, side)) for d in range(side)]
    others = range(1, side)

    w_copies = [
        pltpu.make_async_copy(w_hbm.at[m], raw[m].at[:, pl.ds(0, slots)], w_sem.at[m])
        for m in range(3)
    ]
    for copy in w_copies:
        copy.start()

    barrier = pltpu.get_barrier_semaphore()

    def greet(where):
        pl.semaphore_signal(barrier, inc=1, device_id=where, device_id_type=MESH)

    for d in others:
        pz, py = peers[d]
        for s in (0, 1):
            greet({"ts": pz * side + y, "section": s})
            greet({"ts": z * side + py, "section": s})
    greet({"dp": right})
    greet({"dp": left})
    greet({"section": 1 - sec})

    def remote(src, dst, send, recv, where):
        return pltpu.make_async_remote_copy(
            src_ref=src, dst_ref=dst, send_sem=send, recv_sem=recv,
            device_id=where, device_id_type=MESH,
        )

    def gather_copies(i, phase, q, src=None):
        first = q < 2
        along_y = first == (phase == 0)
        copies = []
        for d in range(side):
            pz, py = peers[d]
            where = {"ts": z * side + py} if along_y else {"ts": pz * side + y}
            if phase == 0:
                dst = g.at[i, z, y, :, cols[q]]
                ref = dst
                if i == 1:
                    ref = src.at[:, cols[q]]
                    where["section"] = 1 - sec
                elif d == 0:
                    continue
            else:
                if d == 0:
                    continue
                ref = g.at[i, z, :, :, cols[q]] if first else g.at[i, :, y, :, cols[q]]
                dst = ref
            copies.append(remote(ref, dst, ag_send.at[i, phase, q, d], ag_recv.at[i, phase, q, d], where))
        return copies

    def gather_first(i, src=None):
        for q in order:
            for copy in gather_copies(i, 0, q, src):
                copy.start()

    def gather_second(i):
        for q in order:
            for copy in gather_copies(i, 0, q, stage):
                copy.wait_recv()
            for copy in gather_copies(i, 1, q):
                copy.start()

    def gather_end(i, q):
        for copy in gather_copies(i, 1, q):
            copy.wait_recv()

    def scatter_copies(use, phase, q):
        first = q < 2
        along_y = first == (phase == 1)
        copies = []
        for d in others:
            pz, py = peers[d]
            where = {"ts": z * side + py} if along_y else {"ts": pz * side + y}
            if phase == 0:
                src = part.at[pz, :, :, cols[q]] if first else part.at[:, py, :, cols[q]]
                dst = rs1.at[use, q, d - 1]
            else:
                src = mid.at[q, py if first else pz]
                dst = rs2.at[use, q, d - 1]
            copies.append(
                remote(src, dst, rs_send.at[use, phase, q, d - 1], rs_recv.at[use, phase, q, d - 1], where)
            )
        return copies

    def scatter_start(use, q):
        for copy in scatter_copies(use, 0, q):
            copy.start()

    def scatter_middle(use):
        for q in order:
            for copy in scatter_copies(use, 0, q):
                copy.wait_recv()
            for i in range(side):
                own = part[z, i, :, cols[q]] if q < 2 else part[i, y, :, cols[q]]
                total = own.astype(F32)
                for d in range(side - 1):
                    total = total + rs1[use, q, d, i].astype(F32)
                mid[q, i] = total.astype(BF16)
            for copy in scatter_copies(use, 1, q):
                copy.start()

    def scatter_end(use):
        totals = []
        for q in range(4):
            for copy in scatter_copies(use, 1, q):
                copy.wait_recv()
            total = mid[q, y if q < 2 else z].astype(F32)
            for d in range(side - 1):
                total = total + rs2[use, q, d].astype(F32)
            totals.append(total)
        return jnp.concatenate(totals, axis=1)

    def scatter_sent(use):
        for phase in (0, 1):
            for q in range(4):
                for copy in scatter_copies(use, phase, q):
                    copy.wait_send()

    def scale_of(values):
        return lax.rsqrt(jnp.mean(values * values, axis=-1, keepdims=True) + EPSILON)

    def normed_of(values, gain):
        return (values * scale_of(values) * gain).astype(BF16)

    def wide(i, q):
        return g[i, :, :, :, cols[q]].reshape(tokens, chunk)

    def act_copy():
        return remote(seg_ref, hop, hop_send.at[0], hop_recv.at[0], {"section": 1})

    def gain_copy():
        return remote(gain_ref, gain_x, hop_send.at[1], hop_recv.at[1], {"section": 0})

    @pl.when(sec == 0)
    def _():
        g[0, z, y] = normed_of(x_ref[...].astype(F32), gain_ref[...])

    @pl.when(sec == 1)
    def _():
        g[0, z, y] = cot_ref[...]

    pl.semaphore_wait(barrier, 4 * (side - 1) + 3)
    gather_first(0)

    @pl.when(sec == 1)
    def _():
        gain_copy().start()

    for m in range(3):
        raw[m][:, slots] = jnp.zeros((hb, block, block), BF16)
    w_copies[0].wait()
    w_copies[1].wait()

    @pl.loop(0, kb)
    def _(k):
        for m in range(2):
            for c in range(hb):
                slot = inv_ref[(m * hb + c) * kb + k]
                at = (2 * c + m) * block
                wgu[pl.ds(k * block, block), at : at + block] = raw[m][c, slot]

    gather_second(0)
    w_copies[2].wait()

    @pl.loop(0, kb)
    def _(k):
        column = pl.ds(pl.multiple_of(k * block, block), block)
        for c in range(hb):
            slot = inv_ref[(2 * hb + c) * kb + k]
            wd[c * block : (c + 1) * block, column] = raw[2][c, slot]

    per_chunk = chunk // block

    def transposed(i, q):
        @pl.loop(0, per_chunk)
        def _(k):
            column = pl.ds(pl.multiple_of(q * chunk + k * block, block), block)
            xt[q * per_chunk + k] = g[i, :, :, :, column].reshape(tokens, block).T

    def delta_blocks(i, q):
        @pl.loop(0, per_chunk)
        def _(k):
            column = pl.ds(pl.multiple_of(q * chunk + k * block, block), block)
            db[q * per_chunk + k] = g[i, :, :, :, column].reshape(tokens, block)

    def down_grad_input(i):
        for n, q in enumerate(order):
            gather_end(i, q)
            term = lax.dot_general(wide(i, q), wd[:, cols[q]], NT, preferred_element_type=F32)
            dhid[...] = term if n == 0 else dhid[...] + term
            delta_blocks(i, q)

    def gate_and_up(i):
        for n, q in enumerate(order):
            gather_end(i, q)
            term = jnp.dot(wide(i, q), wgu[cols[q], :], preferred_element_type=F32)
            gu[...] = term if n == 0 else gu[...] + term
            if n < 3:
                transposed(i, q)

    @pl.when(sec == 0)
    def _():
        gate_and_up(0)

    @pl.when(sec == 1)
    def _():
        down_grad_input(0)
        gather_second(1)
        gate_and_up(1)

    def gate_of(c):
        at = pl.multiple_of(c * 2 * block, 2 * block)
        return gu[:, pl.ds(at, block)], gu[:, pl.ds(pl.multiple_of(at + block, block), block)]

    @pl.loop(0, hb)
    def _(c):
        gate, upper = gate_of(c)
        hid[:, pl.ds(pl.multiple_of(c * block, block), block)] = (
            gate * jax.nn.sigmoid(gate) * upper
        ).astype(BF16)

    def hidden_transposed():
        transposed(sec, order[3])

        @pl.loop(0, hb)
        def _(c):
            hid_t[c] = hid[:, pl.ds(pl.multiple_of(c * block, block), block)].T

    def down(use):
        for q in order:
            out = jnp.dot(hid[...], wd[:, cols[q]], preferred_element_type=F32)
            part[:, :, :, cols[q]] = out.astype(BF16).reshape(side, side, rows, chunk)
            scatter_start(use, q)

    def back(use):
        for q in order:
            out = lax.dot_general(dgu[...], wgu[cols[q], :], NT, preferred_element_type=F32)
            part[:, :, :, cols[q]] = out.astype(BF16).reshape(side, side, rows, chunk)
            scatter_start(use, q)

    def input_grad(values, delta, d_norm):
        scale = scale_of(values)
        scaled = gain_ref[...] * d_norm
        spread = jnp.mean(scaled * values, axis=-1, keepdims=True)
        return (delta + scale * scaled - values * (scale * scale * scale) * spread).astype(BF16)

    def pre_activation_grads():
        @pl.loop(0, hb)
        def _(c):
            gate, upper = gate_of(c)
            d_hidden = dhid[:, pl.ds(pl.multiple_of(c * block, block), block)]
            sig = jax.nn.sigmoid(gate)
            d_gate = d_hidden * upper * sig * (1.0 + gate * (1.0 - sig))
            d_up = d_hidden * gate * sig
            at = pl.multiple_of(c * 2 * block, 2 * block)
            dgu[:, pl.ds(at, block)] = d_gate.astype(BF16)
            dgu[:, pl.ds(pl.multiple_of(at + block, block), block)] = d_up.astype(BF16)

    first, second = slice(0, slots // 2), slice(slots // 2, slots)

    def quarter_of(q):
        return pl.ds(pl.multiple_of(q * quarter, quarter), quarter)

    def ring_first(m, c):
        i = m * hb + c
        q = quarter_of(across)
        return (
            remote(raw[m].at[c, first, q], ex1.at[0, m, c], ex_send.at[0, 0, i], ex_recv.at[0, 0, i], {"dp": right}),
            remote(raw[m].at[c, second, q], ex1.at[1, m, c], ex_send.at[0, 1, i], ex_recv.at[0, 1, i], {"dp": left}),
        )

    def ring_second(m, c):
        i = m * hb + c
        here = pl.ds(0, slots)
        return (
            remote(raw[m].at[c, here, quarter_of(right)], ex2.at[0, m, c], ex_send.at[1, 0, i], ex_recv.at[1, 0, i], {"dp": right}),
            remote(raw[m].at[c, here, quarter_of(left)], ex2.at[1, m, c], ex_send.at[1, 1, i], ex_recv.at[1, 1, i], {"dp": left}),
        )

    def pass_on(m):
        @pl.loop(0, hb)
        def _(c):
            for copy, into, which, arrived in zip(ring_first(m, c), (right, left), (first, second), (0, 1)):
                copy.wait_recv()
                q = quarter_of(into)
                mine = raw[m][c, which, q, :].astype(F32)
                raw[m][c, which, q, :] = (mine + ex1[arrived, m, c].astype(F32)).astype(BF16)
            for copy in ring_second(m, c):
                copy.start()

    def live_of(m, c, j):
        return live_ref[(m * hb + c) * slots + j].astype(F32)

    def down_weight_grads():
        @pl.loop(0, hb)
        def _(c):
            picked = [db[rows_ref[(2 * hb + c) * slots + j]] for j in range(slots)]
            out = jnp.dot(hid_t[c], jnp.concatenate(picked, axis=1), preferred_element_type=F32)
            for j in range(slots):
                raw[2][c, j] = (out[:, j * block : (j + 1) * block] * live_of(2, c, j)).astype(BF16)
            for copy in ring_first(2, c):
                copy.start()

    def weight_grads(m):
        @pl.loop(0, hb)
        def _(c):
            at = pl.multiple_of((2 * c + m) * block, block)
            d_block = dgu[:, pl.ds(at, block)]
            picked = [xt[rows_ref[(m * hb + c) * slots + j]] for j in range(slots)]
            out = jnp.dot(jnp.concatenate(picked, axis=0), d_block, preferred_element_type=F32)
            for j in range(slots):
                raw[m][c, j] = (out[j * block : (j + 1) * block] * live_of(m, c, j)).astype(BF16)
            for copy in ring_first(m, c):
                copy.start()

    @pl.when(sec == 0)
    def _():
        down(0)
        hidden_transposed()
        gain_copy().wait_recv()
        scatter_middle(0)
        act = (x_ref[...].astype(F32) + scatter_end(0)).astype(BF16)
        seg_ref[...] = act
        stage[...] = normed_of(act.astype(F32), gain_x[...])
        gather_first(1, stage)
        act_copy().start()
        scatter_sent(0)
        gather_second(1)
        down_grad_input(1)
        down_weight_grads()
        pre_activation_grads()
        weight_grads(0)
        weight_grads(1)
        pass_on(2)
        back(1)
        pass_on(0)
        scatter_middle(1)
        pass_on(1)
        ing_ref[...] = input_grad(x_ref[...].astype(F32), g[1, z, y].astype(F32), scatter_end(1))
        act_copy().wait_send()

    @pl.when(sec == 1)
    def _():
        pre_activation_grads()
        back(0)
        hidden_transposed()
        down_weight_grads()
        weight_grads(0)
        act_copy().wait_recv()
        scatter_middle(0)
        weight_grads(1)
        ing_ref[...] = input_grad(hop[...].astype(F32), cot_ref[...].astype(F32), scatter_end(0))
        stage[...] = ing_ref[...]
        gather_first(1, stage)
        scatter_sent(0)
        pass_on(2)
        pass_on(0)
        down(1)
        pass_on(1)
        scatter_middle(1)
        seg_ref[...] = (hop[...].astype(F32) + scatter_end(1)).astype(BF16)
        gain_copy().wait_send()

    for m in (2, 0, 1):
        @pl.loop(0, hb)
        def _(c):
            for copy in ring_second(m, c):
                copy.wait_recv()
            total = raw[m][c, pl.ds(0, slots), quarter_of(me), :].astype(F32)
            for way in (0, 1):
                total = total + ex2[way, m, c].astype(F32)
            wg_ref[m, c] = total.astype(BF16)

    scatter_sent(1)
    for i in (0, 1):
        for phase in (0, 1):
            for q in range(4):
                for copy in gather_copies(i, phase, q, stage):
                    copy.wait_send()
    for m in range(3):
        @pl.loop(0, hb)
        def _(c):
            for copy in ring_first(m, c) + ring_second(m, c):
                copy.wait_send()


def shards(inputs, cotangent, gains, weights, block_rows, block_count):
    n_dp, n_ts = lax.axis_size("dp"), lax.axis_size("ts")
    side = math.isqrt(n_ts)
    micro, shard_rows, width = inputs.shape
    rows = micro * shard_rows
    _, _, hb, slots, block, _ = weights.shape
    kb = width // block
    chunk = width // 4
    quarter = block // n_dp
    tokens = rows * n_ts
    lists = block_rows[0]
    live = jnp.arange(slots)[None, None, :] < block_count[0][:, :, None]
    match = (lists[..., None] == jnp.arange(kb)) & live[..., None]
    inverse = jnp.min(jnp.where(match, jnp.arange(slots)[:, None], slots), axis=2)
    vmem = pl.BlockSpec(memory_space=pltpu.VMEM)
    smem = pl.BlockSpec(memory_space=pltpu.SMEM)
    seg, ing, wg = pl.pallas_call(
        functools.partial(kernel, side, n_dp),
        out_shape=(
            jax.ShapeDtypeStruct((rows, width), BF16),
            jax.ShapeDtypeStruct((rows, width), BF16),
            jax.ShapeDtypeStruct((3, hb, slots, quarter, block), BF16),
        ),
        in_specs=[vmem, vmem, vmem, pl.BlockSpec(memory_space=pl.ANY), smem, smem, smem],
        out_specs=(vmem, vmem, vmem),
        scratch_shapes=[
            pltpu.VMEM((hb, slots + 1, block, block), BF16),
            pltpu.VMEM((hb, slots + 1, block, block), BF16),
            pltpu.VMEM((hb, slots + 1, block, block), BF16),
            pltpu.VMEM((width, 2 * hb * block), BF16),
            pltpu.VMEM((hb * block, width), BF16),
            pltpu.VMEM((2, side, side, rows, width), BF16),
            pltpu.VMEM((side, side, rows, width), BF16),
            pltpu.VMEM((2, 4, side - 1, side, rows, chunk), BF16),
            pltpu.VMEM((2, 4, side - 1, rows, chunk), BF16),
            pltpu.VMEM((4, side, rows, chunk), BF16),
            pltpu.VMEM((rows, width), BF16),
            pltpu.VMEM((rows, width), BF16),
            pltpu.VMEM((1, width), F32),
            pltpu.VMEM((tokens, 2 * hb * block), F32),
            pltpu.VMEM((tokens, hb * block), F32),
            pltpu.VMEM((tokens, hb * block), BF16),
            pltpu.VMEM((hb, block, tokens), BF16),
            pltpu.VMEM((tokens, 2 * hb * block), BF16),
            pltpu.VMEM((kb, block, tokens), BF16),
            pltpu.VMEM((kb, tokens, block), BF16),
            pltpu.VMEM((2, 3, hb, slots // 2, quarter, block), BF16),
            pltpu.VMEM((2, 3, hb, slots, quarter, block), BF16),
            pltpu.SemaphoreType.DMA((3,)),
            pltpu.SemaphoreType.DMA((2, 2, 4, side)),
            pltpu.SemaphoreType.DMA((2, 2, 4, side)),
            pltpu.SemaphoreType.DMA((2, 2, 4, side - 1)),
            pltpu.SemaphoreType.DMA((2, 2, 4, side - 1)),
            pltpu.SemaphoreType.DMA((2,)),
            pltpu.SemaphoreType.DMA((2,)),
            pltpu.SemaphoreType.DMA((2, 2, 3 * hb)),
            pltpu.SemaphoreType.DMA((2, 2, 3 * hb)),
        ],
        compiler_params=pltpu.CompilerParams(
            collective_id=0, has_side_effects=True, vmem_limit_bytes=63 * 1024 * 1024
        ),
    )(
        inputs.reshape(rows, width),
        cotangent.reshape(rows, width),
        gains,
        weights[0],
        inverse.reshape(-1).astype(jnp.int32),
        lists.reshape(-1),
        live.reshape(-1).astype(jnp.int32),
    )
    shape = (1, micro, shard_rows, width)
    return seg.reshape(shape), ing.reshape(shape), wg[None]


def solution(mesh):
    in_specs = (
        P(None, ("dp", "ts"), None),
        P(None, ("dp", "ts"), None),
        P("section", None),
        P("section", None, "ts", None, None, None),
        P("section", None, "ts", None),
        P("section", None, "ts"),
    )
    out_specs = (
        P("section", None, ("dp", "ts"), None),
        P("section", None, ("dp", "ts"), None),
        P("section", None, "ts", None, "dp", None),
    )
    return jax.shard_map(shards, mesh=mesh, in_specs=in_specs, out_specs=out_specs, check_vma=False)
```

time: 183 us -> 152 us (0.83)
  Pallas kernels: 171 us -> 140 us
    pallas_call x1, Pallas kernels: 171 us -> 140 us  [shards(): pl.pallas_call(functools.partial(kernel, side, n_dp), out_shape=(jax.Shap...]
where the time goes in v2:
time: 152 us
  Pallas kernels  140 us (92%)
  local copies, waits for them, and re-layouts  10.1 us (7%)
    pallas_call x1, Pallas kernels, shards(): pl.pallas_call(functools.partial(kernel, side, n_dp), out_shape=(jax.Shap...  140 us
    unnamed x4, local copies, waits for them, and re-layouts  7.21 us

profile of v2, /device:TPU:0, one launch (start us, length us, event | category | flops | bytes accessed | tf_op | source)
XLA Modules:
  0.0 151.8 jit_solution(8475050589261499552)
XLA Ops:
  0.6 0.7 copy.15
  1.3 0.7 reduce
  2.1 0.7 reshape_squeeze.3.rows_ref
  2.7 0.1 fusion.1
  2.8 0.7 reshape.37.live_ref
  3.4 0.1 copy.11
  3.6 0.8 copy.12
  4.4 0.1 select_reduce_fusion
  4.5 0.7 reshape.34.inv_ref
  5.2 140.0 %shard_map.85 = (bf16[16,4096]{1,0:T(8,128)(2,1)}, bf16[16,4096]{1,0:T(8,128)(2,1)}, bf16[3,7,12,32,128]{4,3,2,1,0:T(8,128)(2,1)}) custom-call(bf16[16,4096]{1,0:T(8,128)(2,1)} %bitcast.12, bf16[16,4096]{1,0:T(8,128)(2,1)} %bitcast.13, f32[1,4096]{1,0:T(1,128)} %gain_ref.1, bf16[3,7,12,128,128]{4,3,2,1,0:T(8,128)(2,1)} %bitcast.10, s32[672]{0:T(1024)} %reshape.34.inv_ref, ...), custom_call_target="tpu_custom_call" | custom-call | tf_op jit(solution)/shard_map/pallas_call | solution.py:445
  145.2 1.6 %copy.19 = bf16[1,2,8,4096]{3,2,1,0:T(8,128)(2,1)} copy(bf16[1,2,8,4096]{3,2,1,0:T(8,128)(2,1)} %bitcast.15) | data formatting | bytes 262144
  146.8 1.6 %copy.20 = bf16[1,2,8,4096]{3,2,1,0:T(8,128)(2,1)} copy(bf16[1,2,8,4096]{3,2,1,0:T(8,128)(2,1)} %bitcast.14) | data formatting | bytes 262144
  148.4 3.4 %copy.21 = bf16[1,3,7,12,32,128]{5,4,3,2,1,0:T(8,128)(2,1)} copy(bf16[1,3,7,12,32,128]{5,4,3,2,1,0:T(8,128)(2,1)} %bitcast.11) | data formatting | bytes 4128768

commit v3 on v2

--- a/solution.py
+++ b/solution.py
@@ -17,10 +17,11 @@
 
 def kernel(
     side, n_dp,
-    x_ref, cot_ref, gain_ref, w_hbm, inv_ref, rows_ref, live_ref,
+    x_ref, cot_ref, gain_ref, w_hbm, rows_ref, count_ref,
     seg_ref, ing_ref, wg_ref,
-    raw0, raw1, raw2, wgu, wd, g, part, rs1, rs2, mid, hop, stage, gain_x, gu, dhid, hid, hid_t, dgu, xt, db, ex1, ex2,
+    raw0, raw1, raw2, wgu, wd, g, part, rs1, rs2, mid, hop, stage, gain_x, gu, dhid, hid, hid_t, dgu, da, xt, xa, db, ex1, ex2,
     w_sem, ag_send, ag_recv, rs_send, rs_recv, hop_send, hop_recv, ex_send, ex_recv,
+    da_send, da_recv, xa_send, xa_recv, go, inv_v, inv, inv_sem,
 ):
     rows, width = x_ref.shape
     chunk = width // 4
@@ -57,8 +58,8 @@
         for s in (0, 1):
             greet({"ts": pz * side + y, "section": s})
             greet({"ts": z * side + py, "section": s})
-    greet({"dp": right})
-    greet({"dp": left})
+    for other in (right, left, across):
+        greet({"dp": other})
     greet({"section": 1 - sec})
 
     def remote(src, dst, send, recv, where):
@@ -95,8 +96,8 @@
             for copy in gather_copies(i, 0, q, src):
                 copy.start()
 
-    def gather_second(i):
-        for q in order:
+    def gather_second(i, some=order):
+        for q in some:
             for copy in gather_copies(i, 0, q, stage):
                 copy.wait_recv()
             for copy in gather_copies(i, 1, q):
@@ -181,7 +182,7 @@
     def _():
         g[0, z, y] = cot_ref[...]
 
-    pl.semaphore_wait(barrier, 4 * (side - 1) + 3)
+    pl.semaphore_wait(barrier, 4 * (side - 1) + 4)
     gather_first(0)
 
     @pl.when(sec == 1)
@@ -190,6 +191,18 @@
 
     for m in range(3):
         raw[m][:, slots] = jnp.zeros((hb, block, block), BF16)
+
+    lane = lax.broadcasted_iota(jnp.int32, (1, inv_v.shape[1]), 1)
+    for m in range(3):
+        for c in range(hb):
+            found = jnp.full(lane.shape, slots, jnp.int32)
+            for j in range(slots):
+                row = jnp.where(j < count_ref[m, 0, c], rows_ref[m, c, 0, j], -1)
+                found = jnp.where(lane == row, j, found)
+            inv_v[pl.ds(m * hb + c, 1), :] = found
+    inv_copy = pltpu.make_async_copy(inv_v, inv, inv_sem)
+    inv_copy.start()
+    inv_copy.wait()
     w_copies[0].wait()
     w_copies[1].wait()
 
@@ -197,27 +210,47 @@
     def _(k):
         for m in range(2):
             for c in range(hb):
-                slot = inv_ref[(m * hb + c) * kb + k]
+                slot = inv[m * hb + c, k]
                 at = (2 * c + m) * block
                 wgu[pl.ds(k * block, block), at : at + block] = raw[m][c, slot]
 
-    gather_second(0)
+    @pl.when(sec == 0)
+    def _():
+        gather_second(0)
+
     w_copies[2].wait()
 
     @pl.loop(0, kb)
     def _(k):
         column = pl.ds(pl.multiple_of(k * block, block), block)
         for c in range(hb):
-            slot = inv_ref[(2 * hb + c) * kb + k]
+            slot = inv[2 * hb + c, k]
             wd[c * block : (c + 1) * block, column] = raw[2][c, slot]
 
     per_chunk = chunk // block
+
+    def quarter_of(q):
+        return pl.ds(pl.multiple_of(q * quarter, quarter), quarter)
+
+    def normed_copies(q):
+        part_of = pl.ds(q * per_chunk, per_chunk)
+        return [
+            remote(
+                xt.at[part_of, quarter_of(to)], xa.at[n + 1, part_of],
+                xa_send.at[n, q], xa_recv.at[n, q], {"dp": to},
+            )
+            for n, to in enumerate((right, left, across))
+        ]
 
     def transposed(i, q):
         @pl.loop(0, per_chunk)
         def _(k):
             column = pl.ds(pl.multiple_of(q * chunk + k * block, block), block)
             xt[q * per_chunk + k] = g[i, :, :, :, column].reshape(tokens, block).T
+            xa[0, q * per_chunk + k] = xt[q * per_chunk + k, quarter_of(me), :]
+
+        for copy in normed_copies(q):
+            copy.start()
 
     def delta_blocks(i, q):
         @pl.loop(0, per_chunk)
@@ -225,12 +258,15 @@
             column = pl.ds(pl.multiple_of(q * chunk + k * block, block), block)
             db[q * per_chunk + k] = g[i, :, :, :, column].reshape(tokens, block)
 
-    def down_grad_input(i):
-        for n, q in enumerate(order):
+    def down_grad_input(i, some=order):
+        for n, q in enumerate(some):
             gather_end(i, q)
             term = lax.dot_general(wide(i, q), wd[:, cols[q]], NT, preferred_element_type=F32)
-            dhid[...] = term if n == 0 else dhid[...] + term
+            dhid[...] = term if q == order[0] else dhid[...] + term
             delta_blocks(i, q)
+
+    def allow(n):
+        pl.semaphore_signal(go.at[n], inc=1, device_id={"section": 1}, device_id_type=MESH)
 
     def gate_and_up(i):
         for n, q in enumerate(order):
@@ -243,10 +279,16 @@
     @pl.when(sec == 0)
     def _():
         gate_and_up(0)
+        allow(0)
 
     @pl.when(sec == 1)
     def _():
-        down_grad_input(0)
+        pl.semaphore_wait(go.at[0], 1)
+        gather_second(0, order[:2])
+        down_grad_input(0, order[:2])
+        pl.semaphore_wait(go.at[1], 1)
+        gather_second(0, order[2:])
+        down_grad_input(0, order[2:])
         gather_second(1)
         gate_and_up(1)
 
@@ -297,63 +339,90 @@
             at = pl.multiple_of(c * 2 * block, 2 * block)
             dgu[:, pl.ds(at, block)] = d_gate.astype(BF16)
             dgu[:, pl.ds(pl.multiple_of(at + block, block), block)] = d_up.astype(BF16)
+            for copy in grad_copies(c, (0, 1)):
+                copy.start()
+
+    def grad_copies(c, which=(0, 1, 2, 3)):
+        col = pl.ds(pl.multiple_of(c * 2 * block, 2 * block), 2 * block)
+        low, high = pl.ds(0, tokens // 2), pl.ds(tokens // 2, tokens // 2)
+        moves = (
+            (dgu.at[:, col], da.at[0, :, col], right),
+            (dgu.at[:, col], da.at[1, :, col], left),
+            (da.at[0, low, col], da.at[2, low, col], right),
+            (da.at[1, high, col], da.at[2, high, col], left),
+        )
+        return [
+            remote(src, dst, da_send.at[n, c], da_recv.at[n, c], {"dp": to})
+            for n, (src, dst, to) in enumerate(moves)
+            if n in which
+        ]
+
+    def relay():
+        @pl.loop(0, hb)
+        def _(c):
+            for n in (0, 1):
+                grad_copies(c, (n,))[0].wait_recv()
+                grad_copies(c, (n + 2,))[0].start()
 
     first, second = slice(0, slots // 2), slice(slots // 2, slots)
 
-    def quarter_of(q):
-        return pl.ds(pl.multiple_of(q * quarter, quarter), quarter)
-
-    def ring_first(m, c):
-        i = m * hb + c
+    def ring_first(c):
         q = quarter_of(across)
         return (
-            remote(raw[m].at[c, first, q], ex1.at[0, m, c], ex_send.at[0, 0, i], ex_recv.at[0, 0, i], {"dp": right}),
-            remote(raw[m].at[c, second, q], ex1.at[1, m, c], ex_send.at[0, 1, i], ex_recv.at[0, 1, i], {"dp": left}),
+            remote(raw2.at[c, first, q], ex1.at[0, c], ex_send.at[0, 0, c], ex_recv.at[0, 0, c], {"dp": right}),
+            remote(raw2.at[c, second, q], ex1.at[1, c], ex_send.at[0, 1, c], ex_recv.at[0, 1, c], {"dp": left}),
         )
 
-    def ring_second(m, c):
-        i = m * hb + c
+    def ring_second(c):
         here = pl.ds(0, slots)
         return (
-            remote(raw[m].at[c, here, quarter_of(right)], ex2.at[0, m, c], ex_send.at[1, 0, i], ex_recv.at[1, 0, i], {"dp": right}),
-            remote(raw[m].at[c, here, quarter_of(left)], ex2.at[1, m, c], ex_send.at[1, 1, i], ex_recv.at[1, 1, i], {"dp": left}),
+            remote(raw2.at[c, here, quarter_of(right)], ex2.at[0, c], ex_send.at[1, 0, c], ex_recv.at[1, 0, c], {"dp": right}),
+            remote(raw2.at[c, here, quarter_of(left)], ex2.at[1, c], ex_send.at[1, 1, c], ex_recv.at[1, 1, c], {"dp": left}),
         )
 
-    def pass_on(m):
+    def pass_on():
         @pl.loop(0, hb)
         def _(c):
-            for copy, into, which, arrived in zip(ring_first(m, c), (right, left), (first, second), (0, 1)):
+            for copy, into, which, arrived in zip(ring_first(c), (right, left), (first, second), (0, 1)):
                 copy.wait_recv()
                 q = quarter_of(into)
-                mine = raw[m][c, which, q, :].astype(F32)
-                raw[m][c, which, q, :] = (mine + ex1[arrived, m, c].astype(F32)).astype(BF16)
-            for copy in ring_second(m, c):
+                mine = raw2[c, which, q, :].astype(F32)
+                raw2[c, which, q, :] = (mine + ex1[arrived, c].astype(F32)).astype(BF16)
+            for copy in ring_second(c):
                 copy.start()
 
     def live_of(m, c, j):
-        return live_ref[(m * hb + c) * slots + j].astype(F32)
+        return (j < count_ref[m, 0, c]).astype(F32)
 
     def down_weight_grads():
         @pl.loop(0, hb)
         def _(c):
-            picked = [db[rows_ref[(2 * hb + c) * slots + j]] for j in range(slots)]
+            picked = [db[rows_ref[2, c, 0, j]] for j in range(slots)]
             out = jnp.dot(hid_t[c], jnp.concatenate(picked, axis=1), preferred_element_type=F32)
             for j in range(slots):
-                raw[2][c, j] = (out[:, j * block : (j + 1) * block] * live_of(2, c, j)).astype(BF16)
-            for copy in ring_first(2, c):
+                raw2[c, j] = (out[:, j * block : (j + 1) * block] * live_of(2, c, j)).astype(BF16)
+            for copy in ring_first(c):
                 copy.start()
 
-    def weight_grads(m):
+    def weight_grads():
+        for q in range(4):
+            for copy in normed_copies(q):
+                copy.wait_recv()
+
         @pl.loop(0, hb)
         def _(c):
-            at = pl.multiple_of((2 * c + m) * block, block)
-            d_block = dgu[:, pl.ds(at, block)]
-            picked = [xt[rows_ref[(m * hb + c) * slots + j]] for j in range(slots)]
-            out = jnp.dot(jnp.concatenate(picked, axis=0), d_block, preferred_element_type=F32)
-            for j in range(slots):
-                raw[m][c, j] = (out[j * block : (j + 1) * block] * live_of(m, c, j)).astype(BF16)
-            for copy in ring_first(m, c):
-                copy.start()
+            for copy in grad_copies(c, (2, 3)):
+                copy.wait_recv()
+            for m in range(2):
+                col = pl.ds(pl.multiple_of((2 * c + m) * block, block), block)
+                grads = jnp.concatenate([dgu[:, col]] + [da[n, :, col] for n in range(3)], axis=0)
+                picked = []
+                for j in range(slots):
+                    row = rows_ref[m, c, 0, j]
+                    picked.append(jnp.concatenate([xa[n, row] for n in range(4)], axis=1))
+                out = jnp.dot(jnp.concatenate(picked, axis=0), grads, preferred_element_type=F32)
+                for j in range(slots):
+                    wg_ref[m, c, j] = (out[j * quarter : (j + 1) * quarter] * live_of(m, c, j)).astype(BF16)
 
     @pl.when(sec == 0)
     def _():
@@ -361,6 +430,7 @@
         hidden_transposed()
         gain_copy().wait_recv()
         scatter_middle(0)
+        allow(1)
         act = (x_ref[...].astype(F32) + scatter_end(0)).astype(BF16)
         seg_ref[...] = act
         stage[...] = normed_of(act.astype(F32), gain_x[...])
@@ -369,15 +439,14 @@
         scatter_sent(0)
         gather_second(1)
         down_grad_input(1)
+        allow(2)
+        pre_activation_grads()
         down_weight_grads()
-        pre_activation_grads()
-        weight_grads(0)
-        weight_grads(1)
-        pass_on(2)
         back(1)
-        pass_on(0)
+        relay()
+        pass_on()
         scatter_middle(1)
-        pass_on(1)
+        weight_grads()
         ing_ref[...] = input_grad(x_ref[...].astype(F32), g[1, z, y].astype(F32), scatter_end(1))
         act_copy().wait_send()
 
@@ -387,31 +456,29 @@
         back(0)
         hidden_transposed()
         down_weight_grads()
-        weight_grads(0)
         act_copy().wait_recv()
         scatter_middle(0)
-        weight_grads(1)
+        relay()
         ing_ref[...] = input_grad(hop[...].astype(F32), cot_ref[...].astype(F32), scatter_end(0))
         stage[...] = ing_ref[...]
         gather_first(1, stage)
         scatter_sent(0)
-        pass_on(2)
-        pass_on(0)
+        pass_on()
+        weight_grads()
+        pl.semaphore_wait(go.at[2], 1)
         down(1)
-        pass_on(1)
         scatter_middle(1)
         seg_ref[...] = (hop[...].astype(F32) + scatter_end(1)).astype(BF16)
         gain_copy().wait_send()
 
-    for m in (2, 0, 1):
-        @pl.loop(0, hb)
-        def _(c):
-            for copy in ring_second(m, c):
-                copy.wait_recv()
-            total = raw[m][c, pl.ds(0, slots), quarter_of(me), :].astype(F32)
-            for way in (0, 1):
-                total = total + ex2[way, m, c].astype(F32)
-            wg_ref[m, c] = total.astype(BF16)
+    @pl.loop(0, hb)
+    def _(c):
+        for copy in ring_second(c):
+            copy.wait_recv()
+        total = raw2[c, pl.ds(0, slots), quarter_of(me), :].astype(F32)
+        for way in (0, 1):
+            total = total + ex2[way, c].astype(F32)
+        wg_ref[2, c] = total.astype(BF16)
 
     scatter_sent(1)
     for i in (0, 1):
@@ -419,11 +486,29 @@
             for q in range(4):
                 for copy in gather_copies(i, phase, q, stage):
                     copy.wait_send()
+    for q in range(4):
+        for copy in normed_copies(q):
+            copy.wait_send()
+
+    @pl.loop(0, hb)
+    def _(c):
+        for copy in list(ring_first(c) + ring_second(c)) + grad_copies(c):
+            copy.wait_send()
+
+
+def hand_over(seg_in, ing_in, wg_in, seg_out, ing_out, wg_out, seg_at, ing_at, wg_at, sem):
+    pairs = [(seg_in, seg_at, seg_out), (ing_in, ing_at, ing_out)]
     for m in range(3):
-        @pl.loop(0, hb)
-        def _(c):
-            for copy in ring_first(m, c) + ring_second(m, c):
-                copy.wait_send()
+        pairs.append((wg_in.at[0, m], wg_at.at[m], wg_out.at[0, m]))
+    into = [pltpu.make_async_copy(a, b, sem.at[0, n]) for n, (a, b, _) in enumerate(pairs)]
+    out = [pltpu.make_async_copy(b, c, sem.at[1, n]) for n, (_, b, c) in enumerate(pairs)]
+    for copy in into:
+        copy.start()
+    for first, second in zip(into, out):
+        first.wait()
+        second.start()
+    for copy in out:
+        copy.wait()
 
 
 def shards(inputs, cotangent, gains, weights, block_rows, block_count):
@@ -436,10 +521,6 @@
     chunk = width // 4
     quarter = block // n_dp
     tokens = rows * n_ts
-    lists = block_rows[0]
-    live = jnp.arange(slots)[None, None, :] < block_count[0][:, :, None]
-    match = (lists[..., None] == jnp.arange(kb)) & live[..., None]
-    inverse = jnp.min(jnp.where(match, jnp.arange(slots)[:, None], slots), axis=2)
     vmem = pl.BlockSpec(memory_space=pltpu.VMEM)
     smem = pl.BlockSpec(memory_space=pltpu.SMEM)
     seg, ing, wg = pl.pallas_call(
@@ -449,7 +530,7 @@
             jax.ShapeDtypeStruct((rows, width), BF16),
             jax.ShapeDtypeStruct((3, hb, slots, quarter, block), BF16),
         ),
-        in_specs=[vmem, vmem, vmem, pl.BlockSpec(memory_space=pl.ANY), smem, smem, smem],
+        in_specs=[vmem, vmem, vmem, pl.BlockSpec(memory_space=pl.ANY), smem, smem],
         out_specs=(vmem, vmem, vmem),
         scratch_shapes=[
             pltpu.VMEM((hb, slots + 1, block, block), BF16),
@@ -470,10 +551,12 @@
             pltpu.VMEM((tokens, hb * block), BF16),
             pltpu.VMEM((hb, block, tokens), BF16),
             pltpu.VMEM((tokens, 2 * hb * block), BF16),
+            pltpu.VMEM((3, tokens, 2 * hb * block), BF16),
             pltpu.VMEM((kb, block, tokens), BF16),
+            pltpu.VMEM((4, kb, quarter, tokens), BF16),
             pltpu.VMEM((kb, tokens, block), BF16),
-            pltpu.VMEM((2, 3, hb, slots // 2, quarter, block), BF16),
-            pltpu.VMEM((2, 3, hb, slots, quarter, block), BF16),
+            pltpu.VMEM((2, hb, slots // 2, quarter, block), BF16),
+            pltpu.VMEM((2, hb, slots, quarter, block), BF16),
             pltpu.SemaphoreType.DMA((3,)),
             pltpu.SemaphoreType.DMA((2, 2, 4, side)),
             pltpu.SemaphoreType.DMA((2, 2, 4, side)),
@@ -481,8 +564,16 @@
             pltpu.SemaphoreType.DMA((2, 2, 4, side - 1)),
             pltpu.SemaphoreType.DMA((2,)),
             pltpu.SemaphoreType.DMA((2,)),
-            pltpu.SemaphoreType.DMA((2, 2, 3 * hb)),
-            pltpu.SemaphoreType.DMA((2, 2, 3 * hb)),
+            pltpu.SemaphoreType.DMA((2, 2, hb)),
+            pltpu.SemaphoreType.DMA((2, 2, hb)),
+            pltpu.SemaphoreType.DMA((4, hb)),
+            pltpu.SemaphoreType.DMA((4, hb)),
+            pltpu.SemaphoreType.DMA((3, 4)),
+            pltpu.SemaphoreType.DMA((3, 4)),
+            pltpu.SemaphoreType.REGULAR((3,)),
+            pltpu.VMEM((-(-3 * hb // 8) * 8, 128), jnp.int32),
+            pltpu.SMEM((-(-3 * hb // 8) * 8, 128), jnp.int32),
+            pltpu.SemaphoreType.DMA,
         ],
         compiler_params=pltpu.CompilerParams(
             collective_id=0, has_side_effects=True, vmem_limit_bytes=63 * 1024 * 1024
@@ -492,12 +583,24 @@
         cotangent.reshape(rows, width),
         gains,
         weights[0],
-        inverse.reshape(-1).astype(jnp.int32),
-        lists.reshape(-1),
-        live.reshape(-1).astype(jnp.int32),
+        block_rows.transpose(1, 2, 0, 3),
+        block_count.transpose(1, 0, 2),
     )
     shape = (1, micro, shard_rows, width)
-    return seg.reshape(shape), ing.reshape(shape), wg[None]
+    results = (seg.reshape(shape), ing.reshape(shape), wg[None])
+    hbm = pl.BlockSpec(memory_space=pl.ANY)
+    return pl.pallas_call(
+        hand_over,
+        out_shape=tuple(jax.ShapeDtypeStruct(x.shape, x.dtype) for x in results),
+        in_specs=[hbm] * 3,
+        out_specs=(hbm,) * 3,
+        scratch_shapes=[
+            pltpu.VMEM(shape, BF16),
+            pltpu.VMEM(shape, BF16),
+            pltpu.VMEM(wg.shape, BF16),
+            pltpu.SemaphoreType.DMA((2, 5)),
+        ],
+    )(*results)
 
 
 def solution(mesh):

time: 152 us -> 127 us (0.84)
  Pallas kernels: 140 us -> 126 us
  local copies, waits for them, and re-layouts: 10.1 us -> 0 us
    pallas_call x1, Pallas kernels: 140 us -> 124 us  [shards(): pl.pallas_call(functools.partial(kernel, side, n_dp), out_shape=(jax.Shap...]
    unnamed x4 -> x0, local copies, waits for them, and re-layouts: 7.21 us -> none
    pallas_call x0 -> x1, Pallas kernels: none -> 2.63 us  [shards(): pl.pallas_call(hand_over, out_shape=tuple((jax.ShapeDtypeStruct(x.shape,...]
where the time goes in v3:
time: 127 us
  Pallas kernels  126 us (99%)
    pallas_call x1, Pallas kernels, shards(): pl.pallas_call(functools.partial(kernel, side, n_dp), out_shape=(jax.Shap...  124 us
    pallas_call x1, Pallas kernels, shards(): pl.pallas_call(hand_over, out_shape=tuple((jax.ShapeDtypeStruct(x.shape,...  2.63 us

profile of v3, /device:TPU:0, one launch (start us, length us, event | category | flops | bytes accessed | tf_op | source)
XLA Modules:
  0.0 127.1 jit_solution(6839468131354774864)
XLA Ops:
  0.6 123.6 %shard_map.85 = (bf16[16,4096]{1,0:T(8,128)(2,1)}, bf16[16,4096]{1,0:T(8,128)(2,1)}, bf16[3,7,12,32,128]{4,3,2,1,0:T(8,128)(2,1)}) custom-call(bf16[16,4096]{1,0:T(8,128)(2,1)} %bitcast.10, bf16[16,4096]{1,0:T(8,128)(2,1)} %bitcast.11, f32[1,4096]{1,0:T(1,128)} %gain_ref.1, bf16[3,7,12,128,128]{4,3,2,1,0:T(8,128)(2,1)} %bitcast.8, s32[3,7,1,12]{3,2,1,0:T(1,128)} %bitcast.14, ...), custom_call_target="tpu_custom_call" | custom-call | tf_op jit(solution)/shard_map/pallas_call | solution.py:526
  124.3 2.6 %shard_map.86 = (bf16[1,2,8,4096]{3,2,1,0:T(8,128)(2,1)}, bf16[1,2,8,4096]{3,2,1,0:T(8,128)(2,1)}, bf16[1,3,7,12,32,128]{5,4,3,2,1,0:T(8,128)(2,1)}) custom-call(bf16[1,2,8,4096]{3,2,1,0:T(8,128)(2,1)} %bitcast.12, bf16[1,2,8,4096]{3,2,1,0:T(8,128)(2,1)} %bitcast.13, bf16[1,3,7,12,32,128]{5,4,3,2,1,0:T(8,128)(2,1)} %bitcast.9), custom_call_target="tpu_custom_call" | custom-call | tf_op jit(solution)/shard_map/pallas_call | solution.py:592

commit v4 on v3

--- a/solution.py
+++ b/solution.py
@@ -13,6 +13,11 @@
 F32 = jnp.float32
 BF16 = jnp.bfloat16
 NT = (((1,), (1,)), ((), ()))
+
+
+def groups_of(hb):
+    step = 2
+    return [(lo, min(lo + step, hb)) for lo in range(0, hb, step)]
 
 
 def kernel(
@@ -37,7 +42,9 @@
     across = lax.rem(me + 2, n_dp)
     raw = (raw0, raw1, raw2)
     cols = [slice(q * chunk, (q + 1) * chunk) for q in range(4)]
+    halves = [slice(h * 2 * chunk, (h + 1) * 2 * chunk) for h in range(2)]
     order = (0, 2, 1, 3)
+    groups = groups_of(hb)
     peers = [(lax.rem(z + d, side), lax.rem(y + d, side)) for d in range(side)]
     others = range(1, side)
 
@@ -45,8 +52,8 @@
         pltpu.make_async_copy(w_hbm.at[m], raw[m].at[:, pl.ds(0, slots)], w_sem.at[m])
         for m in range(3)
     ]
-    for copy in w_copies:
-        copy.start()
+    for m in (2, 0, 1):
+        w_copies[m].start()
 
     barrier = pltpu.get_barrier_semaphore()
 
@@ -203,6 +210,19 @@
     inv_copy = pltpu.make_async_copy(inv_v, inv, inv_sem)
     inv_copy.start()
     inv_copy.wait()
+    w_copies[2].wait()
+
+    @pl.loop(0, kb)
+    def _(k):
+        column = pl.ds(pl.multiple_of(k * block, block), block)
+        for c in range(hb):
+            slot = inv[2 * hb + c, k]
+            wd[c * block : (c + 1) * block, column] = raw[2][c, slot]
+
+    @pl.when(sec == 0)
+    def _():
+        gather_second(0)
+
     w_copies[0].wait()
     w_copies[1].wait()
 
@@ -213,19 +233,6 @@
                 slot = inv[m * hb + c, k]
                 at = (2 * c + m) * block
                 wgu[pl.ds(k * block, block), at : at + block] = raw[m][c, slot]
-
-    @pl.when(sec == 0)
-    def _():
-        gather_second(0)
-
-    w_copies[2].wait()
-
-    @pl.loop(0, kb)
-    def _(k):
-        column = pl.ds(pl.multiple_of(k * block, block), block)
-        for c in range(hb):
-            slot = inv[2 * hb + c, k]
-            wd[c * block : (c + 1) * block, column] = raw[2][c, slot]
 
     per_chunk = chunk // block
 
@@ -273,7 +280,7 @@
             gather_end(i, q)
             term = jnp.dot(wide(i, q), wgu[cols[q], :], preferred_element_type=F32)
             gu[...] = term if n == 0 else gu[...] + term
-            if n < 3:
+            if i == 1 and n < 3:
                 transposed(i, q)
 
     @pl.when(sec == 0)
@@ -296,15 +303,17 @@
         at = pl.multiple_of(c * 2 * block, 2 * block)
         return gu[:, pl.ds(at, block)], gu[:, pl.ds(pl.multiple_of(at + block, block), block)]
 
-    @pl.loop(0, hb)
-    def _(c):
-        gate, upper = gate_of(c)
-        hid[:, pl.ds(pl.multiple_of(c * block, block), block)] = (
-            gate * jax.nn.sigmoid(gate) * upper
-        ).astype(BF16)
-
-    def hidden_transposed():
-        transposed(sec, order[3])
+    def hidden():
+        @pl.loop(0, hb)
+        def _(c):
+            gate, upper = gate_of(c)
+            hid[:, pl.ds(pl.multiple_of(c * block, block), block)] = (
+                gate * jax.nn.sigmoid(gate) * upper
+            ).astype(BF16)
+
+    def hidden_transposed(some):
+        for q in some:
+            transposed(sec, q)
 
         @pl.loop(0, hb)
         def _(c):
@@ -328,8 +337,8 @@
         spread = jnp.mean(scaled * values, axis=-1, keepdims=True)
         return (delta + scale * scaled - values * (scale * scale * scale) * spread).astype(BF16)
 
-    def pre_activation_grads():
-        @pl.loop(0, hb)
+    def pre_activation_grads(n):
+        @pl.loop(*groups[n])
         def _(c):
             gate, upper = gate_of(c)
             d_hidden = dhid[:, pl.ds(pl.multiple_of(c * block, block), block)]
@@ -339,11 +348,10 @@
             at = pl.multiple_of(c * 2 * block, 2 * block)
             dgu[:, pl.ds(at, block)] = d_gate.astype(BF16)
             dgu[:, pl.ds(pl.multiple_of(at + block, block), block)] = d_up.astype(BF16)
-            for copy in grad_copies(c, (0, 1)):
-                copy.start()
-
-    def grad_copies(c, which=(0, 1, 2, 3)):
-        col = pl.ds(pl.multiple_of(c * 2 * block, 2 * block), 2 * block)
+
+    def grad_copies(group, which):
+        lo, hi = groups[group]
+        col = slice(lo * 2 * block, hi * 2 * block)
         low, high = pl.ds(0, tokens // 2), pl.ds(tokens // 2, tokens // 2)
         moves = (
             (dgu.at[:, col], da.at[0, :, col], right),
@@ -352,82 +360,93 @@
             (da.at[1, high, col], da.at[2, high, col], left),
         )
         return [
-            remote(src, dst, da_send.at[n, c], da_recv.at[n, c], {"dp": to})
+            remote(src, dst, da_send.at[n, group], da_recv.at[n, group], {"dp": to})
             for n, (src, dst, to) in enumerate(moves)
             if n in which
         ]
 
+    def grads_out(group):
+        for copy in grad_copies(group, (0, 1)):
+            copy.start()
+
     def relay():
-        @pl.loop(0, hb)
-        def _(c):
+        for group in range(len(groups)):
             for n in (0, 1):
-                grad_copies(c, (n,))[0].wait_recv()
-                grad_copies(c, (n + 2,))[0].start()
+                grad_copies(group, (n,))[0].wait_recv()
+                grad_copies(group, (n + 2,))[0].start()
 
     first, second = slice(0, slots // 2), slice(slots // 2, slots)
 
-    def ring_first(c):
-        q = quarter_of(across)
+    def ring_first(group):
+        q, here = quarter_of(across), slice(*groups[group])
         return (
-            remote(raw2.at[c, first, q], ex1.at[0, c], ex_send.at[0, 0, c], ex_recv.at[0, 0, c], {"dp": right}),
-            remote(raw2.at[c, second, q], ex1.at[1, c], ex_send.at[0, 1, c], ex_recv.at[0, 1, c], {"dp": left}),
+            remote(raw2.at[here, first, q], ex1.at[0, here], ex_send.at[0, 0, group], ex_recv.at[0, 0, group], {"dp": right}),
+            remote(raw2.at[here, second, q], ex1.at[1, here], ex_send.at[0, 1, group], ex_recv.at[0, 1, group], {"dp": left}),
         )
 
-    def ring_second(c):
-        here = pl.ds(0, slots)
+    def ring_second(group):
+        here, every = slice(*groups[group]), slice(0, slots)
         return (
-            remote(raw2.at[c, here, quarter_of(right)], ex2.at[0, c], ex_send.at[1, 0, c], ex_recv.at[1, 0, c], {"dp": right}),
-            remote(raw2.at[c, here, quarter_of(left)], ex2.at[1, c], ex_send.at[1, 1, c], ex_recv.at[1, 1, c], {"dp": left}),
+            remote(raw2.at[here, every, quarter_of(right)], ex2.at[0, here], ex_send.at[1, 0, group], ex_recv.at[1, 0, group], {"dp": right}),
+            remote(raw2.at[here, every, quarter_of(left)], ex2.at[1, here], ex_send.at[1, 1, group], ex_recv.at[1, 1, group], {"dp": left}),
         )
 
     def pass_on():
-        @pl.loop(0, hb)
-        def _(c):
-            for copy, into, which, arrived in zip(ring_first(c), (right, left), (first, second), (0, 1)):
+        for group in range(len(groups)):
+            for copy in ring_first(group):
                 copy.wait_recv()
-                q = quarter_of(into)
-                mine = raw2[c, which, q, :].astype(F32)
-                raw2[c, which, q, :] = (mine + ex1[arrived, c].astype(F32)).astype(BF16)
-            for copy in ring_second(c):
+
+            @pl.loop(*groups[group])
+            def _(c):
+                for into, which, arrived in ((right, first, 0), (left, second, 1)):
+                    q = quarter_of(into)
+                    mine = raw2[c, which, q, :].astype(F32)
+                    raw2[c, which, q, :] = (mine + ex1[arrived, c].astype(F32)).astype(BF16)
+
+            for copy in ring_second(group):
                 copy.start()
 
     def live_of(m, c, j):
         return (j < count_ref[m, 0, c]).astype(F32)
 
     def down_weight_grads():
-        @pl.loop(0, hb)
-        def _(c):
-            picked = [db[rows_ref[2, c, 0, j]] for j in range(slots)]
-            out = jnp.dot(hid_t[c], jnp.concatenate(picked, axis=1), preferred_element_type=F32)
-            for j in range(slots):
-                raw2[c, j] = (out[:, j * block : (j + 1) * block] * live_of(2, c, j)).astype(BF16)
-            for copy in ring_first(c):
+        for group in range(len(groups)):
+            @pl.loop(*groups[group])
+            def _(c):
+                picked = [db[rows_ref[2, c, 0, j]] for j in range(slots)]
+                out = jnp.dot(hid_t[c], jnp.concatenate(picked, axis=1), preferred_element_type=F32)
+                for j in range(slots):
+                    raw2[c, j] = (out[:, j * block : (j + 1) * block] * live_of(2, c, j)).astype(BF16)
+
+            for copy in ring_first(group):
                 copy.start()
 
     def weight_grads():
         for q in range(4):
             for copy in normed_copies(q):
                 copy.wait_recv()
-
-        @pl.loop(0, hb)
-        def _(c):
-            for copy in grad_copies(c, (2, 3)):
+        for group in range(len(groups)):
+            for copy in grad_copies(group, (2, 3)):
                 copy.wait_recv()
-            for m in range(2):
-                col = pl.ds(pl.multiple_of((2 * c + m) * block, block), block)
-                grads = jnp.concatenate([dgu[:, col]] + [da[n, :, col] for n in range(3)], axis=0)
-                picked = []
-                for j in range(slots):
-                    row = rows_ref[m, c, 0, j]
-                    picked.append(jnp.concatenate([xa[n, row] for n in range(4)], axis=1))
-                out = jnp.dot(jnp.concatenate(picked, axis=0), grads, preferred_element_type=F32)
-                for j in range(slots):
-                    wg_ref[m, c, j] = (out[j * quarter : (j + 1) * quarter] * live_of(m, c, j)).astype(BF16)
+
+            @pl.loop(*groups[group])
+            def _(c):
+                for m in range(2):
+                    col = pl.ds(pl.multiple_of((2 * c + m) * block, block), block)
+                    grads = jnp.concatenate([dgu[:, col]] + [da[n, :, col] for n in range(3)], axis=0)
+                    picked = []
+                    for j in range(slots):
+                        row = rows_ref[m, c, 0, j]
+                        picked.append(jnp.concatenate([xa[n, row] for n in range(4)], axis=1))
+                    out = jnp.dot(jnp.concatenate(picked, axis=0), grads, preferred_element_type=F32)
+                    for j in range(slots):
+                        wg_ref[m, c, j] = (out[j * quarter : (j + 1) * quarter] * live_of(m, c, j)).astype(BF16)
 
     @pl.when(sec == 0)
     def _():
+        hidden()
         down(0)
-        hidden_transposed()
+        hidden_transposed(order)
         gain_copy().wait_recv()
         scatter_middle(0)
         allow(1)
@@ -440,7 +459,9 @@
         gather_second(1)
         down_grad_input(1)
         allow(2)
-        pre_activation_grads()
+        for group in range(len(groups)):
+            pre_activation_grads(group)
+            grads_out(group)
         down_weight_grads()
         back(1)
         relay()
@@ -452,9 +473,12 @@
 
     @pl.when(sec == 1)
     def _():
-        pre_activation_grads()
+        for group in range(len(groups)):
+            pre_activation_grads(group)
+            grads_out(group)
         back(0)
-        hidden_transposed()
+        hidden()
+        hidden_transposed(order[3:])
         down_weight_grads()
         act_copy().wait_recv()
         scatter_middle(0)
@@ -471,14 +495,16 @@
         seg_ref[...] = (hop[...].astype(F32) + scatter_end(1)).astype(BF16)
         gain_copy().wait_send()
 
-    @pl.loop(0, hb)
-    def _(c):
-        for copy in ring_second(c):
+    for group in range(len(groups)):
+        for copy in ring_second(group):
             copy.wait_recv()
-        total = raw2[c, pl.ds(0, slots), quarter_of(me), :].astype(F32)
-        for way in (0, 1):
-            total = total + ex2[way, c].astype(F32)
-        wg_ref[2, c] = total.astype(BF16)
+
+        @pl.loop(*groups[group])
+        def _(c):
+            total = raw2[c, pl.ds(0, slots), quarter_of(me), :].astype(F32)
+            for way in (0, 1):
+                total = total + ex2[way, c].astype(F32)
+            wg_ref[2, c] = total.astype(BF16)
 
     scatter_sent(1)
     for i in (0, 1):
@@ -489,10 +515,8 @@
     for q in range(4):
         for copy in normed_copies(q):
             copy.wait_send()
-
-    @pl.loop(0, hb)
-    def _(c):
-        for copy in list(ring_first(c) + ring_second(c)) + grad_copies(c):
+    for group in range(len(groups)):
+        for copy in list(ring_first(group) + ring_second(group)) + grad_copies(group, (0, 1, 2, 3)):
             copy.wait_send()
 
 
@@ -564,10 +588,10 @@
             pltpu.SemaphoreType.DMA((2, 2, 4, side - 1)),
             pltpu.SemaphoreType.DMA((2,)),
             pltpu.SemaphoreType.DMA((2,)),
-            pltpu.SemaphoreType.DMA((2, 2, hb)),
-            pltpu.SemaphoreType.DMA((2, 2, hb)),
-            pltpu.SemaphoreType.DMA((4, hb)),
-            pltpu.SemaphoreType.DMA((4, hb)),
+            pltpu.SemaphoreType.DMA((2, 2, len(groups_of(hb)))),
+            pltpu.SemaphoreType.DMA((2, 2, len(groups_of(hb)))),
+            pltpu.SemaphoreType.DMA((4, len(groups_of(hb)))),
+            pltpu.SemaphoreType.DMA((4, len(groups_of(hb)))),
             pltpu.SemaphoreType.DMA((3, 4)),
             pltpu.SemaphoreType.DMA((3, 4)),
             pltpu.SemaphoreType.REGULAR((3,)),

time: 127 us -> 125 us (0.984)
  Pallas kernels: 126 us -> 124 us
    pallas_call x1, Pallas kernels: 124 us -> 121 us  [shards(): pl.pallas_call(functools.partial(kernel, side, n_dp), out_shape=(jax.Shap...]
where the time goes in v4:
time: 125 us
  Pallas kernels  124 us (99%)
    pallas_call x1, Pallas kernels, shards(): pl.pallas_call(functools.partial(kernel, side, n_dp), out_shape=(jax.Shap...  121 us
    pallas_call x1, Pallas kernels, shards(): pl.pallas_call(hand_over, out_shape=tuple((jax.ShapeDtypeStruct(x.shape,...  2.63 us

profile of v4, /device:TPU:0, one launch (start us, length us, event | category | flops | bytes accessed | tf_op | source)
XLA Modules:
  0.0 124.8 jit_solution(2271892750433044438)
XLA Ops:
  0.6 121.3 %shard_map.85 = (bf16[16,4096]{1,0:T(8,128)(2,1)}, bf16[16,4096]{1,0:T(8,128)(2,1)}, bf16[3,7,12,32,128]{4,3,2,1,0:T(8,128)(2,1)}) custom-call(bf16[16,4096]{1,0:T(8,128)(2,1)} %bitcast.10, bf16[16,4096]{1,0:T(8,128)(2,1)} %bitcast.11, f32[1,4096]{1,0:T(1,128)} %gain_ref.1, bf16[3,7,12,128,128]{4,3,2,1,0:T(8,128)(2,1)} %bitcast.8, s32[3,7,1,12]{3,2,1,0:T(1,128)} %bitcast.14, ...), custom_call_target="tpu_custom_call" | custom-call | tf_op jit(solution)/shard_map/pallas_call | solution.py:550
  122.0 2.6 %shard_map.86 = (bf16[1,2,8,4096]{3,2,1,0:T(8,128)(2,1)}, bf16[1,2,8,4096]{3,2,1,0:T(8,128)(2,1)}, bf16[1,3,7,12,32,128]{5,4,3,2,1,0:T(8,128)(2,1)}) custom-call(bf16[1,2,8,4096]{3,2,1,0:T(8,128)(2,1)} %bitcast.12, bf16[1,2,8,4096]{3,2,1,0:T(8,128)(2,1)} %bitcast.13, bf16[1,3,7,12,32,128]{5,4,3,2,1,0:T(8,128)(2,1)} %bitcast.9), custom_call_target="tpu_custom_call" | custom-call | tf_op jit(solution)/shard_map/pallas_call | solution.py:616
